TPU v7x, 512 devices: a whole 4x4x16 slice. The times are simulated.
512 devices in a mesh: outer: 16 (over z_lo, core), inner: 32 (over x, z_hi, y).
Axes of the slice: x: 4, y: 4, z: 16 (z_hi: 2, z_lo: 8; z = z_hi * 8 + z_lo), core: 2. Of those that a mesh axis runs over, the one named last changes fastest.
Arguments:
- q_heads: bfloat16 [16, 4096, 1024], P('outer', 'inner'), may hold values from -6 to 6
- k_head: bfloat16 [16, 4096, 128], P('outer', 'inner'), may hold values from -6 to 6
- v_head: bfloat16 [16, 4096, 128], P('outer', 'inner'), may hold values from -6 to 6
- out_grad: bfloat16 [16, 4096, 1024], P('outer', 'inner'), may hold values from -6 to 6
- weight_codes: int32 [16, 4096], P('outer', 'inner'), may hold values from 1 to 16
- bounds: int32 [16, 2], P('outer'), may hold values from 1024 to 3071, as said below
- block_order: int32 [64], replicated, may hold values from 0 to 63, each once
Outputs:
- q_grad: bfloat16 [16, 4096, 1024], P('outer', 'inner')
- k_grad: bfloat16 [16, 4096, 128], P('outer', 'inner')
- v_grad: bfloat16 [16, 4096, 128], P('outer', 'inner')
- bias_grad: float32 [1280], replicated
Inputs may be any that keep to these rules, and one draw needn't show every extreme that they name: `block_order`: a permutation: each value once. `bounds`: first column in [1024, 2048), second in [2048, 3072).
All inputs are finite; a program needn't handle non-finite values.
Results may differ from a plain program's by a relative error of at most 0.02.
Values may be sent and summed in bfloat16 or wider, within the bound.
A program may use at most 64 MiB of HBM per device.

v0:
```python
import math

import jax
import jax.numpy as jnp
from jax import lax
from jax.sharding import PartitionSpec as P

NEG_SCORE = -1e30


def from_behind(block, axis, distance):
    devices = range(lax.axis_size(axis))
    route = [((i - distance) % len(devices), i) for i in devices]
    return lax.ppermute(block, axis, route)


def visible(q_pos, k_pos, pair_start, second_start):
    later = q_pos[:, None] >= k_pos[None, :]
    crossed = (
        (k_pos[None, :] >= pair_start)
        & (k_pos[None, :] < second_start)
        & (q_pos[:, None] >= second_start)
    )
    return later & jnp.logical_not(crossed)


def keep_state(current):
    return current


def per_device(q_heads, k_head, v_head, out_grad, weight_codes, bounds, block_order):
    row_count = k_head.shape[1]
    head_width = k_head.shape[2]
    head_count = q_heads.shape[2] // head_width
    half_rows = row_count // 2
    inv_scale = 1.0 / math.sqrt(head_width)
    cycle_size = lax.axis_size("inner")
    cycle_place = lax.axis_index("inner")
    pair_start = bounds[0, 0]
    second_start = bounds[0, 1]
    offsets = jnp.arange(half_rows, dtype=jnp.int32)
    queries = q_heads[0].reshape(row_count, head_count, head_width)
    token_scale = weight_codes[0].astype(jnp.float32) / 16.0
    weighted = (out_grad[0].astype(jnp.float32) * token_scale[:, None]).astype(jnp.bfloat16)
    weighted = weighted.reshape(row_count, head_count, head_width)

    def block_start(anchor, which):
        return lax.dynamic_index_in_dim(block_order, 2 * anchor + which, keepdims=False) * half_rows

    own_starts = (block_start(cycle_place, 0), block_start(cycle_place, 1))

    def forward_tile(states, moving, anchor):
        result = []
        for q_part in range(2):
            current_state = states[q_part]
            for k_part in range(2):
                key_start = block_start(anchor, k_part)

                def forward_update(current, q_part=q_part, k_part=k_part, key_start=key_start):
                    running, totals, summed = current
                    q_block = queries[q_part * half_rows : (q_part + 1) * half_rows]
                    k_block = moving[0, k_part * half_rows : (k_part + 1) * half_rows]
                    v_block = moving[1, k_part * half_rows : (k_part + 1) * half_rows]
                    scores = (
                        jnp.einsum(
                            "qhd,kd->hqk", q_block, k_block, preferred_element_type=jnp.float32
                        )
                        * inv_scale
                    )
                    allowed = visible(
                        own_starts[q_part] + offsets, key_start + offsets, pair_start, second_start
                    )[None]
                    newest = jnp.maximum(
                        running, jnp.max(jnp.where(allowed, scores, NEG_SCORE), axis=2)
                    )
                    factor = jnp.exp(running - newest)
                    weights = jnp.where(allowed, jnp.exp(scores - newest[:, :, None]), 0.0)
                    totals = totals * factor + jnp.sum(weights, axis=2)
                    summed = summed * factor.T[:, :, None] + jnp.einsum(
                        "hqk,kd->qhd",
                        weights,
                        v_block.astype(jnp.float32),
                        preferred_element_type=jnp.float32,
                    )
                    return (newest, totals, summed)

                current_state = lax.cond(
                    key_start <= own_starts[q_part], forward_update, keep_state, current_state
                )
            result.append(current_state)
        return tuple(result)

    key_vals = jnp.stack([k_head[0], v_head[0]])
    start_state = (
        jnp.full((head_count, half_rows), NEG_SCORE, jnp.float32),
        jnp.zeros((head_count, half_rows), jnp.float32),
        jnp.zeros((half_rows, head_count, head_width), jnp.float32),
    )

    def forward_hop(hop_index, carry):
        moving, states = carry
        anchor = (cycle_place - hop_index) % cycle_size
        states = forward_tile(states, moving, anchor)
        moving = from_behind(moving, "inner", 1)
        return (moving, states)

    moving, states = lax.fori_loop(
        0, cycle_size, forward_hop, (key_vals, (start_state, start_state))
    )
    log_totals = []
    deltas = []
    for q_part in range(2):
        running, totals, summed = states[q_part]
        log_totals.append(running + jnp.log(totals))
        attn_out = summed / totals.T[:, :, None]
        g_block = weighted[q_part * half_rows : (q_part + 1) * half_rows]
        deltas.append(jnp.sum(g_block.astype(jnp.float32) * attn_out, axis=2).T)

    def backward_tile(q_grads, key_grads, moving, anchor):
        q_grads = list(q_grads)
        for q_part in range(2):
            for k_part in range(2):
                key_start = block_start(anchor, k_part)

                def backward_update(current, q_part=q_part, k_part=k_part, key_start=key_start):
                    q_acc, k_acc, v_acc = current
                    q_block = queries[q_part * half_rows : (q_part + 1) * half_rows]
                    g_block = weighted[q_part * half_rows : (q_part + 1) * half_rows]
                    k_block = moving[0, k_part * half_rows : (k_part + 1) * half_rows]
                    v_block = moving[1, k_part * half_rows : (k_part + 1) * half_rows]
                    scores = (
                        jnp.einsum(
                            "qhd,kd->hqk", q_block, k_block, preferred_element_type=jnp.float32
                        )
                        * inv_scale
                    )
                    allowed = visible(
                        own_starts[q_part] + offsets, key_start + offsets, pair_start, second_start
                    )[None]
                    probs = jnp.where(
                        allowed, jnp.exp(scores - log_totals[q_part][:, :, None]), 0.0
                    )
                    probs_low = probs.astype(jnp.bfloat16)
                    v_acc = v_acc + jnp.einsum(
                        "hqk,qhd->kd", probs_low, g_block, preferred_element_type=jnp.float32
                    )
                    dprobs = jnp.einsum(
                        "qhd,kd->hqk", g_block, v_block, preferred_element_type=jnp.float32
                    )
                    dscores = (probs * (dprobs - deltas[q_part][:, :, None])).astype(jnp.bfloat16)
                    q_acc = (
                        q_acc
                        + jnp.einsum(
                            "hqk,kd->qhd", dscores, k_block, preferred_element_type=jnp.float32
                        )
                        * inv_scale
                    )
                    k_acc = (
                        k_acc
                        + jnp.einsum(
                            "hqk,qhd->kd", dscores, q_block, preferred_element_type=jnp.float32
                        )
                        * inv_scale
                    )
                    return (q_acc, k_acc, v_acc)

                current = (q_grads[q_part], key_grads[0, k_part], key_grads[1, k_part])
                q_new, k_new, v_new = lax.cond(
                    key_start <= own_starts[q_part], backward_update, keep_state, current
                )
                q_grads[q_part] = q_new
                key_grads = key_grads.at[0, k_part].set(k_new).at[1, k_part].set(v_new)
        return (tuple(q_grads), key_grads)

    zero_grads = jnp.zeros((2, 2, half_rows, head_width), jnp.float32)
    zero_query = jnp.zeros((half_rows, head_count, head_width), jnp.float32)

    def back_hop(hop_index, carry):
        moving, key_grads, q_grads = carry
        anchor = (cycle_place - hop_index) % cycle_size
        q_grads, key_grads = backward_tile(q_grads, key_grads, moving, anchor)
        moving = from_behind(moving, "inner", 1)
        key_grads = from_behind(key_grads, "inner", 1)
        return (moving, key_grads, q_grads)

    moving, key_grads, q_grads = lax.fori_loop(
        0, cycle_size, back_hop, (key_vals, zero_grads, (zero_query, zero_query))
    )
    q_full = jnp.concatenate(q_grads, axis=0)
    k_full = jnp.concatenate([key_grads[0, 0], key_grads[0, 1]], axis=0)
    v_full = jnp.concatenate([key_grads[1, 0], key_grads[1, 1]], axis=0)
    local_sums = jnp.concatenate(
        [jnp.sum(q_full, axis=0).reshape(-1), jnp.sum(k_full, axis=0), jnp.sum(v_full, axis=0)]
    )
    pair_tokens = lax.axis_size("outer") * cycle_size * row_count
    bias_grad = lax.psum(local_sums, ("outer", "inner")) / math.sqrt(pair_tokens)
    q_out = q_full.reshape(1, row_count, head_count * head_width).astype(jnp.bfloat16)
    return (q_out, k_full[None].astype(jnp.bfloat16), v_full[None].astype(jnp.bfloat16), bias_grad)


def solution(mesh):
    return jax.shard_map(
        per_device,
        mesh=mesh,
        in_specs=(
            P("outer", "inner", None),
            P("outer", "inner", None),
            P("outer", "inner", None),
            P("outer", "inner", None),
            P("outer", "inner"),
            P("outer", None),
            P(),
        ),
        out_specs=(
            P("outer", "inner", None),
            P("outer", "inner", None),
            P("outer", "inner", None),
            P(),
        ),
        check_vma=False,
    )
```

profile of v0, /device:TPU:1, one launch (start us, length us, event | category | flops | bytes accessed | tf_op | source)
XLA Modules:
  0.0 1988.6 jit_solution(16190551904570077126)
XLA Ops:
  7.2 612.9 %while.61 = (s32[]{:T(128)}, bf16[2,128,128]{2,1,0:T(8,128)(2,1)S(1)}, f32[8,64]{1,0:T(8,128)S(1)}, f32[8,64]{1,0:T(8,128)S(1)}, f32[64,8,128]{2,0,1:T(8,128)S(1...) while((s32[]{:T(128)}, ...), condition=%wide.region_17.18_spmd.clone.clone, body=%wide.region_0.17_spmd.clone.clone.sunk | while | flops 68754976 | bytes 4940162 | solution.py:107
  622.4 1173.9 %while.62 = (s32[]{:T(128)}, bf16[2,128,128]{2,1,0:T(8,128)(2,1)S(1)}, f32[2,2,64,128]{3,2,1,0:T(8,128)S(1)}, f32[64,8,128]{2,0,1:T(8,128)S(1)}, f32[64,8,128]{2...) while((s32[]{:T(128)}, ...), condition=%wide.region_29.30_spmd.clone.clone, body=%wide.region_20.29_spmd.clone.clone.sunk | while | flops 169379360 | bytes 11166290 | solution.py:186
  638.9 15.8 collective-permute-done.2
  669.5 17.4 collective-permute-done.2
  702.4 16.3 collective-permute-done.2
  814.3 25.1 %collective-permute-done.2 = f32[2,2,64,128]{3,2,1,0:T(8,128)S(1)} collective-permute-done((f32[2,2,64,128]{3,2,1,0:T(8,128)S(1)}, f32[2,2,64,128]{3,2,1,0:T(8,128)S(1)}, u32[]{:S(2)}, u32[]{:S(2)}) %collective-permute-start.2) | collective-permute-done | bytes 131104 | tf_op jit(solution)/shard_map/while/body/eval_jaxpr/ppermute | solution.py:14
  851.6 27.6 %collective-permute-done.2 = f32[2,2,64,128]{3,2,1,0:T(8,128)S(1)} collective-permute-done((f32[2,2,64,128]{3,2,1,0:T(8,128)S(1)}, f32[2,2,64,128]{3,2,1,0:T(8,128)S(1)}, u32[]{:S(2)}, u32[]{:S(2)}) %collective-permute-start.2) | collective-permute-done | bytes 131104 | tf_op jit(solution)/shard_map/while/body/eval_jaxpr/ppermute | solution.py:14
  894.6 18.2 collective-permute-done.2
  930.0 16.5 collective-permute-done.2
  961.6 19.5 collective-permute-done.2
  991.5 16.3 collective-permute-done.2
  1032.9 28.0 %collective-permute-done.2 = f32[2,2,64,128]{3,2,1,0:T(8,128)S(1)} collective-permute-done((f32[2,2,64,128]{3,2,1,0:T(8,128)S(1)}, f32[2,2,64,128]{3,2,1,0:T(8,128)S(1)}, u32[]{:S(2)}, u32[]{:S(2)}) %collective-permute-start.2) | collective-permute-done | bytes 131104 | tf_op jit(solution)/shard_map/while/body/eval_jaxpr/ppermute | solution.py:14
  1071.3 15.2 collective-permute-done.2
  1110.6 26.5 %collective-permute-done.2 = f32[2,2,64,128]{3,2,1,0:T(8,128)S(1)} collective-permute-done((f32[2,2,64,128]{3,2,1,0:T(8,128)S(1)}, f32[2,2,64,128]{3,2,1,0:T(8,128)S(1)}, u32[]{:S(2)}, u32[]{:S(2)}) %collective-permute-start.2) | collective-permute-done | bytes 131104 | tf_op jit(solution)/shard_map/while/body/eval_jaxpr/ppermute | solution.py:14
  1150.1 26.0 %collective-permute-done.2 = f32[2,2,64,128]{3,2,1,0:T(8,128)S(1)} collective-permute-done((f32[2,2,64,128]{3,2,1,0:T(8,128)S(1)}, f32[2,2,64,128]{3,2,1,0:T(8,128)S(1)}, u32[]{:S(2)}, u32[]{:S(2)}) %collective-permute-start.2) | collective-permute-done | bytes 131104 | tf_op jit(solution)/shard_map/while/body/eval_jaxpr/ppermute | solution.py:14
  1191.4 24.6 %collective-permute-done.2 = f32[2,2,64,128]{3,2,1,0:T(8,128)S(1)} collective-permute-done((f32[2,2,64,128]{3,2,1,0:T(8,128)S(1)}, f32[2,2,64,128]{3,2,1,0:T(8,128)S(1)}, u32[]{:S(2)}, u32[]{:S(2)}) %collective-permute-start.2) | collective-permute-done | bytes 131104 | tf_op jit(solution)/shard_map/while/body/eval_jaxpr/ppermute | solution.py:14
  1228.9 28.2 %collective-permute-done.2 = f32[2,2,64,128]{3,2,1,0:T(8,128)S(1)} collective-permute-done((f32[2,2,64,128]{3,2,1,0:T(8,128)S(1)}, f32[2,2,64,128]{3,2,1,0:T(8,128)S(1)}, u32[]{:S(2)}, u32[]{:S(2)}) %collective-permute-start.2) | collective-permute-done | bytes 131104 | tf_op jit(solution)/shard_map/while/body/eval_jaxpr/ppermute | solution.py:14
  1272.5 24.9 %collective-permute-done.2 = f32[2,2,64,128]{3,2,1,0:T(8,128)S(1)} collective-permute-done((f32[2,2,64,128]{3,2,1,0:T(8,128)S(1)}, f32[2,2,64,128]{3,2,1,0:T(8,128)S(1)}, u32[]{:S(2)}, u32[]{:S(2)}) %collective-permute-start.2) | collective-permute-done | bytes 131104 | tf_op jit(solution)/shard_map/while/body/eval_jaxpr/ppermute | solution.py:14
  1307.8 22.9 %collective-permute-done.2 = f32[2,2,64,128]{3,2,1,0:T(8,128)S(1)} collective-permute-done((f32[2,2,64,128]{3,2,1,0:T(8,128)S(1)}, f32[2,2,64,128]{3,2,1,0:T(8,128)S(1)}, u32[]{:S(2)}, u32[]{:S(2)}) %collective-permute-start.2) | collective-permute-done | bytes 131104 | tf_op jit(solution)/shard_map/while/body/eval_jaxpr/ppermute | solution.py:14
  1348.4 24.7 %collective-permute-done.2 = f32[2,2,64,128]{3,2,1,0:T(8,128)S(1)} collective-permute-done((f32[2,2,64,128]{3,2,1,0:T(8,128)S(1)}, f32[2,2,64,128]{3,2,1,0:T(8,128)S(1)}, u32[]{:S(2)}, u32[]{:S(2)}) %collective-permute-start.2) | collective-permute-done | bytes 131104 | tf_op jit(solution)/shard_map/while/body/eval_jaxpr/ppermute | solution.py:14
  1391.1 19.3 collective-permute-done.2
  1425.6 23.0 %collective-permute-done.2 = f32[2,2,64,128]{3,2,1,0:T(8,128)S(1)} collective-permute-done((f32[2,2,64,128]{3,2,1,0:T(8,128)S(1)}, f32[2,2,64,128]{3,2,1,0:T(8,128)S(1)}, u32[]{:S(2)}, u32[]{:S(2)}) %collective-permute-start.2) | collective-permute-done | bytes 131104 | tf_op jit(solution)/shard_map/while/body/eval_jaxpr/ppermute | solution.py:14
  1463.9 25.0 %collective-permute-done.2 = f32[2,2,64,128]{3,2,1,0:T(8,128)S(1)} collective-permute-done((f32[2,2,64,128]{3,2,1,0:T(8,128)S(1)}, f32[2,2,64,128]{3,2,1,0:T(8,128)S(1)}, u32[]{:S(2)}, u32[]{:S(2)}) %collective-permute-start.2) | collective-permute-done | bytes 131104 | tf_op jit(solution)/shard_map/while/body/eval_jaxpr/ppermute | solution.py:14
  1499.4 26.3 %collective-permute-done.2 = f32[2,2,64,128]{3,2,1,0:T(8,128)S(1)} collective-permute-done((f32[2,2,64,128]{3,2,1,0:T(8,128)S(1)}, f32[2,2,64,128]{3,2,1,0:T(8,128)S(1)}, u32[]{:S(2)}, u32[]{:S(2)}) %collective-permute-start.2) | collective-permute-done | bytes 131104 | tf_op jit(solution)/shard_map/while/body/eval_jaxpr/ppermute | solution.py:14
  1543.6 23.5 %collective-permute-done.2 = f32[2,2,64,128]{3,2,1,0:T(8,128)S(1)} collective-permute-done((f32[2,2,64,128]{3,2,1,0:T(8,128)S(1)}, f32[2,2,64,128]{3,2,1,0:T(8,128)S(1)}, u32[]{:S(2)}, u32[]{:S(2)}) %collective-permute-start.2) | collective-permute-done | bytes 131104 | tf_op jit(solution)/shard_map/while/body/eval_jaxpr/ppermute | solution.py:14
  1579.9 28.2 %collective-permute-done.2 = f32[2,2,64,128]{3,2,1,0:T(8,128)S(1)} collective-permute-done((f32[2,2,64,128]{3,2,1,0:T(8,128)S(1)}, f32[2,2,64,128]{3,2,1,0:T(8,128)S(1)}, u32[]{:S(2)}, u32[]{:S(2)}) %collective-permute-start.2) | collective-permute-done | bytes 131104 | tf_op jit(solution)/shard_map/while/body/eval_jaxpr/ppermute | solution.py:14
  1617.8 18.7 collective-permute-done.2
  1656.1 28.2 %collective-permute-done.2 = f32[2,2,64,128]{3,2,1,0:T(8,128)S(1)} collective-permute-done((f32[2,2,64,128]{3,2,1,0:T(8,128)S(1)}, f32[2,2,64,128]{3,2,1,0:T(8,128)S(1)}, u32[]{:S(2)}, u32[]{:S(2)}) %collective-permute-start.2) | collective-permute-done | bytes 131104 | tf_op jit(solution)/shard_map/while/body/eval_jaxpr/ppermute | solution.py:14
  1704.7 21.2 %collective-permute-done.2 = f32[2,2,64,128]{3,2,1,0:T(8,128)S(1)} collective-permute-done((f32[2,2,64,128]{3,2,1,0:T(8,128)S(1)}, f32[2,2,64,128]{3,2,1,0:T(8,128)S(1)}, u32[]{:S(2)}, u32[]{:S(2)}) %collective-permute-start.2) | collective-permute-done | bytes 131104 | tf_op jit(solution)/shard_map/while/body/eval_jaxpr/ppermute | solution.py:14
  1745.6 15.3 collective-permute-done.2
  1775.8 19.8 collective-permute-done.2
  1796.4 189.9 %psum.7 = f32[1280]{0:T(1024)S(1)} all-reduce(f32[1280]{0:T(1024)S(1)} %pad_maximum_fusion.3), channel_id=1, replica_groups=mesh['outer'=16,'inner'=32] {'outer','inner'}, use_global_device_ids=true, to_apply=%region_36.37 | all-reduce | flops 1280 | bytes 10240 | tf_op jit(solution)/shard_map/psum | solution.py:196
  (1927 shorter events, 1368.6 us)
Async XLA Ops:
  810.4 29.0 %collective-permute-start.2 = (f32[2,2,64,128]{3,2,1,0:T(8,128)S(1)}, f32[2,2,64,128]{3,2,1,0:T(8,128)S(1)}, u32[]{:S(2)}, u32[]{:S(2)}) collective-permute-start(f32[2,2,64,128]{3,2,1,0:T(8,128)S(1)} %constant_dynamic-update-slice_fusion.25), channel_id=1, source_target_pairs={{31,0},{0,1},{1,2},{2,3},{3,4},{4,5},{5,6},{6,7},{7,8},{8,9},{9,10... | collective-permute-start | bytes 393224 | tf_op jit(solution)/shard_map/while/body/eval_jaxpr/ppermute | solution.py:14
  812.3 27.7 %collective-permute-start.1 = (bf16[2,128,128]{2,1,0:T(8,128)(2,1)S(1)}, bf16[2,128,128]{2,1,0:T(8,128)(2,1)S(1)}, u32[]{:S(2)}, u32[]{:S(2)}) collective-permute-start(bf16[2,128,128]{2,1,0:T(8,128)(2,1)S(1)} %copy.189), channel_id=1, source_target_pairs={{31,0},{0,1},{1,2},{2,3},{3,4},{4,5},{5,6},{6,7},{7,8},{8,9},{9,10... | collective-permute-start | bytes 196616 | tf_op jit(solution)/shard_map/while/body/eval_jaxpr/ppermute | solution.py:14
  847.7 31.4 %collective-permute-start.2 = (f32[2,2,64,128]{3,2,1,0:T(8,128)S(1)}, f32[2,2,64,128]{3,2,1,0:T(8,128)S(1)}, u32[]{:S(2)}, u32[]{:S(2)}) collective-permute-start(f32[2,2,64,128]{3,2,1,0:T(8,128)S(1)} %constant_dynamic-update-slice_fusion.25), channel_id=1, source_target_pairs={{31,0},{0,1},{1,2},{2,3},{3,4},{4,5},{5,6},{6,7},{7,8},{8,9},{9,10... | collective-permute-start | bytes 393224 | tf_op jit(solution)/shard_map/while/body/eval_jaxpr/ppermute | solution.py:14
  849.7 30.9 %collective-permute-start.1 = (bf16[2,128,128]{2,1,0:T(8,128)(2,1)S(1)}, bf16[2,128,128]{2,1,0:T(8,128)(2,1)S(1)}, u32[]{:S(2)}, u32[]{:S(2)}) collective-permute-start(bf16[2,128,128]{2,1,0:T(8,128)(2,1)S(1)} %copy.189), channel_id=1, source_target_pairs={{31,0},{0,1},{1,2},{2,3},{3,4},{4,5},{5,6},{6,7},{7,8},{8,9},{9,10... | collective-permute-start | bytes 196616 | tf_op jit(solution)/shard_map/while/body/eval_jaxpr/ppermute | solution.py:14
  989.6 29.3 %collective-permute-start.1 = (bf16[2,128,128]{2,1,0:T(8,128)(2,1)S(1)}, bf16[2,128,128]{2,1,0:T(8,128)(2,1)S(1)}, u32[]{:S(2)}, u32[]{:S(2)}) collective-permute-start(bf16[2,128,128]{2,1,0:T(8,128)(2,1)S(1)} %copy.189), channel_id=1, source_target_pairs={{31,0},{0,1},{1,2},{2,3},{3,4},{4,5},{5,6},{6,7},{7,8},{8,9},{9,10... | collective-permute-start | bytes 196616 | tf_op jit(solution)/shard_map/while/body/eval_jaxpr/ppermute | solution.py:14
  1029.0 31.8 %collective-permute-start.2 = (f32[2,2,64,128]{3,2,1,0:T(8,128)S(1)}, f32[2,2,64,128]{3,2,1,0:T(8,128)S(1)}, u32[]{:S(2)}, u32[]{:S(2)}) collective-permute-start(f32[2,2,64,128]{3,2,1,0:T(8,128)S(1)} %constant_dynamic-update-slice_fusion.25), channel_id=1, source_target_pairs={{31,0},{0,1},{1,2},{2,3},{3,4},{4,5},{5,6},{6,7},{7,8},{8,9},{9,10... | collective-permute-start | bytes 393224 | tf_op jit(solution)/shard_map/while/body/eval_jaxpr/ppermute | solution.py:14
  1030.9 31.3 %collective-permute-start.1 = (bf16[2,128,128]{2,1,0:T(8,128)(2,1)S(1)}, bf16[2,128,128]{2,1,0:T(8,128)(2,1)S(1)}, u32[]{:S(2)}, u32[]{:S(2)}) collective-permute-start(bf16[2,128,128]{2,1,0:T(8,128)(2,1)S(1)} %copy.189), channel_id=1, source_target_pairs={{31,0},{0,1},{1,2},{2,3},{3,4},{4,5},{5,6},{6,7},{7,8},{8,9},{9,10... | collective-permute-start | bytes 196616 | tf_op jit(solution)/shard_map/while/body/eval_jaxpr/ppermute | solution.py:14
  1069.3 29.8 %collective-permute-start.1 = (bf16[2,128,128]{2,1,0:T(8,128)(2,1)S(1)}, bf16[2,128,128]{2,1,0:T(8,128)(2,1)S(1)}, u32[]{:S(2)}, u32[]{:S(2)}) collective-permute-start(bf16[2,128,128]{2,1,0:T(8,128)(2,1)S(1)} %copy.189), channel_id=1, source_target_pairs={{31,0},{0,1},{1,2},{2,3},{3,4},{4,5},{5,6},{6,7},{7,8},{8,9},{9,10... | collective-permute-start | bytes 196616 | tf_op jit(solution)/shard_map/while/body/eval_jaxpr/ppermute | solution.py:14
  1106.8 30.4 %collective-permute-start.2 = (f32[2,2,64,128]{3,2,1,0:T(8,128)S(1)}, f32[2,2,64,128]{3,2,1,0:T(8,128)S(1)}, u32[]{:S(2)}, u32[]{:S(2)}) collective-permute-start(f32[2,2,64,128]{3,2,1,0:T(8,128)S(1)} %constant_dynamic-update-slice_fusion.25), channel_id=1, source_target_pairs={{31,0},{0,1},{1,2},{2,3},{3,4},{4,5},{5,6},{6,7},{7,8},{8,9},{9,10... | collective-permute-start | bytes 393224 | tf_op jit(solution)/shard_map/while/body/eval_jaxpr/ppermute | solution.py:14
  1108.7 29.9 %collective-permute-start.1 = (bf16[2,128,128]{2,1,0:T(8,128)(2,1)S(1)}, bf16[2,128,128]{2,1,0:T(8,128)(2,1)S(1)}, u32[]{:S(2)}, u32[]{:S(2)}) collective-permute-start(bf16[2,128,128]{2,1,0:T(8,128)(2,1)S(1)} %copy.189), channel_id=1, source_target_pairs={{31,0},{0,1},{1,2},{2,3},{3,4},{4,5},{5,6},{6,7},{7,8},{8,9},{9,10... | collective-permute-start | bytes 196616 | tf_op jit(solution)/shard_map/while/body/eval_jaxpr/ppermute | solution.py:14
  1146.2 29.9 %collective-permute-start.2 = (f32[2,2,64,128]{3,2,1,0:T(8,128)S(1)}, f32[2,2,64,128]{3,2,1,0:T(8,128)S(1)}, u32[]{:S(2)}, u32[]{:S(2)}) collective-permute-start(f32[2,2,64,128]{3,2,1,0:T(8,128)S(1)} %constant_dynamic-update-slice_fusion.25), channel_id=1, source_target_pairs={{31,0},{0,1},{1,2},{2,3},{3,4},{4,5},{5,6},{6,7},{7,8},{8,9},{9,10... | collective-permute-start | bytes 393224 | tf_op jit(solution)/shard_map/while/body/eval_jaxpr/ppermute | solution.py:14
  1148.2 29.3 %collective-permute-start.1 = (bf16[2,128,128]{2,1,0:T(8,128)(2,1)S(1)}, bf16[2,128,128]{2,1,0:T(8,128)(2,1)S(1)}, u32[]{:S(2)}, u32[]{:S(2)}) collective-permute-start(bf16[2,128,128]{2,1,0:T(8,128)(2,1)S(1)} %copy.189), channel_id=1, source_target_pairs={{31,0},{0,1},{1,2},{2,3},{3,4},{4,5},{5,6},{6,7},{7,8},{8,9},{9,10... | collective-permute-start | bytes 196616 | tf_op jit(solution)/shard_map/while/body/eval_jaxpr/ppermute | solution.py:14
  1187.6 28.5 %collective-permute-start.2 = (f32[2,2,64,128]{3,2,1,0:T(8,128)S(1)}, f32[2,2,64,128]{3,2,1,0:T(8,128)S(1)}, u32[]{:S(2)}, u32[]{:S(2)}) collective-permute-start(f32[2,2,64,128]{3,2,1,0:T(8,128)S(1)} %constant_dynamic-update-slice_fusion.25), channel_id=1, source_target_pairs={{31,0},{0,1},{1,2},{2,3},{3,4},{4,5},{5,6},{6,7},{7,8},{8,9},{9,10... | collective-permute-start | bytes 393224 | tf_op jit(solution)/shard_map/while/body/eval_jaxpr/ppermute | solution.py:14
  1189.5 27.8 %collective-permute-start.1 = (bf16[2,128,128]{2,1,0:T(8,128)(2,1)S(1)}, bf16[2,128,128]{2,1,0:T(8,128)(2,1)S(1)}, u32[]{:S(2)}, u32[]{:S(2)}) collective-permute-start(bf16[2,128,128]{2,1,0:T(8,128)(2,1)S(1)} %copy.189), channel_id=1, source_target_pairs={{31,0},{0,1},{1,2},{2,3},{3,4},{4,5},{5,6},{6,7},{7,8},{8,9},{9,10... | collective-permute-start | bytes 196616 | tf_op jit(solution)/shard_map/while/body/eval_jaxpr/ppermute | solution.py:14
  1225.0 32.1 %collective-permute-start.2 = (f32[2,2,64,128]{3,2,1,0:T(8,128)S(1)}, f32[2,2,64,128]{3,2,1,0:T(8,128)S(1)}, u32[]{:S(2)}, u32[]{:S(2)}) collective-permute-start(f32[2,2,64,128]{3,2,1,0:T(8,128)S(1)} %constant_dynamic-update-slice_fusion.25), channel_id=1, source_target_pairs={{31,0},{0,1},{1,2},{2,3},{3,4},{4,5},{5,6},{6,7},{7,8},{8,9},{9,10... | collective-permute-start | bytes 393224 | tf_op jit(solution)/shard_map/while/body/eval_jaxpr/ppermute | solution.py:14
  1226.9 31.5 %collective-permute-start.1 = (bf16[2,128,128]{2,1,0:T(8,128)(2,1)S(1)}, bf16[2,128,128]{2,1,0:T(8,128)(2,1)S(1)}, u32[]{:S(2)}, u32[]{:S(2)}) collective-permute-start(bf16[2,128,128]{2,1,0:T(8,128)(2,1)S(1)} %copy.189), channel_id=1, source_target_pairs={{31,0},{0,1},{1,2},{2,3},{3,4},{4,5},{5,6},{6,7},{7,8},{8,9},{9,10... | collective-permute-start | bytes 196616 | tf_op jit(solution)/shard_map/while/body/eval_jaxpr/ppermute | solution.py:14
  1268.6 28.7 %collective-permute-start.2 = (f32[2,2,64,128]{3,2,1,0:T(8,128)S(1)}, f32[2,2,64,128]{3,2,1,0:T(8,128)S(1)}, u32[]{:S(2)}, u32[]{:S(2)}) collective-permute-start(f32[2,2,64,128]{3,2,1,0:T(8,128)S(1)} %constant_dynamic-update-slice_fusion.25), channel_id=1, source_target_pairs={{31,0},{0,1},{1,2},{2,3},{3,4},{4,5},{5,6},{6,7},{7,8},{8,9},{9,10... | collective-permute-start | bytes 393224 | tf_op jit(solution)/shard_map/while/body/eval_jaxpr/ppermute | solution.py:14
  1270.6 28.2 %collective-permute-start.1 = (bf16[2,128,128]{2,1,0:T(8,128)(2,1)S(1)}, bf16[2,128,128]{2,1,0:T(8,128)(2,1)S(1)}, u32[]{:S(2)}, u32[]{:S(2)}) collective-permute-start(bf16[2,128,128]{2,1,0:T(8,128)(2,1)S(1)} %copy.189), channel_id=1, source_target_pairs={{31,0},{0,1},{1,2},{2,3},{3,4},{4,5},{5,6},{6,7},{7,8},{8,9},{9,10... | collective-permute-start | bytes 196616 | tf_op jit(solution)/shard_map/while/body/eval_jaxpr/ppermute | solution.py:14
  1305.9 31.0 %collective-permute-start.1 = (bf16[2,128,128]{2,1,0:T(8,128)(2,1)S(1)}, bf16[2,128,128]{2,1,0:T(8,128)(2,1)S(1)}, u32[]{:S(2)}, u32[]{:S(2)}) collective-permute-start(bf16[2,128,128]{2,1,0:T(8,128)(2,1)S(1)} %copy.189), channel_id=1, source_target_pairs={{31,0},{0,1},{1,2},{2,3},{3,4},{4,5},{5,6},{6,7},{7,8},{8,9},{9,10... | collective-permute-start | bytes 196616 | tf_op jit(solution)/shard_map/while/body/eval_jaxpr/ppermute | solution.py:14
  1344.5 28.6 %collective-permute-start.2 = (f32[2,2,64,128]{3,2,1,0:T(8,128)S(1)}, f32[2,2,64,128]{3,2,1,0:T(8,128)S(1)}, u32[]{:S(2)}, u32[]{:S(2)}) collective-permute-start(f32[2,2,64,128]{3,2,1,0:T(8,128)S(1)} %constant_dynamic-update-slice_fusion.25), channel_id=1, source_target_pairs={{31,0},{0,1},{1,2},{2,3},{3,4},{4,5},{5,6},{6,7},{7,8},{8,9},{9,10... | collective-permute-start | bytes 393224 | tf_op jit(solution)/shard_map/while/body/eval_jaxpr/ppermute | solution.py:14
  1346.5 28.1 %collective-permute-start.1 = (bf16[2,128,128]{2,1,0:T(8,128)(2,1)S(1)}, bf16[2,128,128]{2,1,0:T(8,128)(2,1)S(1)}, u32[]{:S(2)}, u32[]{:S(2)}) collective-permute-start(bf16[2,128,128]{2,1,0:T(8,128)(2,1)S(1)} %copy.189), channel_id=1, source_target_pairs={{31,0},{0,1},{1,2},{2,3},{3,4},{4,5},{5,6},{6,7},{7,8},{8,9},{9,10... | collective-permute-start | bytes 196616 | tf_op jit(solution)/shard_map/while/body/eval_jaxpr/ppermute | solution.py:14
  1421.7 26.9 %collective-permute-start.2 = (f32[2,2,64,128]{3,2,1,0:T(8,128)S(1)}, f32[2,2,64,128]{3,2,1,0:T(8,128)S(1)}, u32[]{:S(2)}, u32[]{:S(2)}) collective-permute-start(f32[2,2,64,128]{3,2,1,0:T(8,128)S(1)} %constant_dynamic-update-slice_fusion.25), channel_id=1, source_target_pairs={{31,0},{0,1},{1,2},{2,3},{3,4},{4,5},{5,6},{6,7},{7,8},{8,9},{9,10... | collective-permute-start | bytes 393224 | tf_op jit(solution)/shard_map/while/body/eval_jaxpr/ppermute | solution.py:14
  1460.1 28.9 %collective-permute-start.2 = (f32[2,2,64,128]{3,2,1,0:T(8,128)S(1)}, f32[2,2,64,128]{3,2,1,0:T(8,128)S(1)}, u32[]{:S(2)}, u32[]{:S(2)}) collective-permute-start(f32[2,2,64,128]{3,2,1,0:T(8,128)S(1)} %constant_dynamic-update-slice_fusion.25), channel_id=1, source_target_pairs={{31,0},{0,1},{1,2},{2,3},{3,4},{4,5},{5,6},{6,7},{7,8},{8,9},{9,10... | collective-permute-start | bytes 393224 | tf_op jit(solution)/shard_map/while/body/eval_jaxpr/ppermute | solution.py:14
  1462.0 28.4 %collective-permute-start.1 = (bf16[2,128,128]{2,1,0:T(8,128)(2,1)S(1)}, bf16[2,128,128]{2,1,0:T(8,128)(2,1)S(1)}, u32[]{:S(2)}, u32[]{:S(2)}) collective-permute-start(bf16[2,128,128]{2,1,0:T(8,128)(2,1)S(1)} %copy.189), channel_id=1, source_target_pairs={{31,0},{0,1},{1,2},{2,3},{3,4},{4,5},{5,6},{6,7},{7,8},{8,9},{9,10... | collective-permute-start | bytes 196616 | tf_op jit(solution)/shard_map/while/body/eval_jaxpr/ppermute | solution.py:14
  1495.5 30.1 %collective-permute-start.2 = (f32[2,2,64,128]{3,2,1,0:T(8,128)S(1)}, f32[2,2,64,128]{3,2,1,0:T(8,128)S(1)}, u32[]{:S(2)}, u32[]{:S(2)}) collective-permute-start(f32[2,2,64,128]{3,2,1,0:T(8,128)S(1)} %constant_dynamic-update-slice_fusion.25), channel_id=1, source_target_pairs={{31,0},{0,1},{1,2},{2,3},{3,4},{4,5},{5,6},{6,7},{7,8},{8,9},{9,10... | collective-permute-start | bytes 393224 | tf_op jit(solution)/shard_map/while/body/eval_jaxpr/ppermute | solution.py:14
  1497.4 29.6 %collective-permute-start.1 = (bf16[2,128,128]{2,1,0:T(8,128)(2,1)S(1)}, bf16[2,128,128]{2,1,0:T(8,128)(2,1)S(1)}, u32[]{:S(2)}, u32[]{:S(2)}) collective-permute-start(bf16[2,128,128]{2,1,0:T(8,128)(2,1)S(1)} %copy.189), channel_id=1, source_target_pairs={{31,0},{0,1},{1,2},{2,3},{3,4},{4,5},{5,6},{6,7},{7,8},{8,9},{9,10... | collective-permute-start | bytes 196616 | tf_op jit(solution)/shard_map/while/body/eval_jaxpr/ppermute | solution.py:14
  1539.7 27.3 %collective-permute-start.2 = (f32[2,2,64,128]{3,2,1,0:T(8,128)S(1)}, f32[2,2,64,128]{3,2,1,0:T(8,128)S(1)}, u32[]{:S(2)}, u32[]{:S(2)}) collective-permute-start(f32[2,2,64,128]{3,2,1,0:T(8,128)S(1)} %constant_dynamic-update-slice_fusion.25), channel_id=1, source_target_pairs={{31,0},{0,1},{1,2},{2,3},{3,4},{4,5},{5,6},{6,7},{7,8},{8,9},{9,10... | collective-permute-start | bytes 393224 | tf_op jit(solution)/shard_map/while/body/eval_jaxpr/ppermute | solution.py:14
  1541.7 26.7 %collective-permute-start.1 = (bf16[2,128,128]{2,1,0:T(8,128)(2,1)S(1)}, bf16[2,128,128]{2,1,0:T(8,128)(2,1)S(1)}, u32[]{:S(2)}, u32[]{:S(2)}) collective-permute-start(bf16[2,128,128]{2,1,0:T(8,128)(2,1)S(1)} %copy.189), channel_id=1, source_target_pairs={{31,0},{0,1},{1,2},{2,3},{3,4},{4,5},{5,6},{6,7},{7,8},{8,9},{9,10... | collective-permute-start | bytes 196616 | tf_op jit(solution)/shard_map/while/body/eval_jaxpr/ppermute | solution.py:14
  1576.0 32.1 %collective-permute-start.2 = (f32[2,2,64,128]{3,2,1,0:T(8,128)S(1)}, f32[2,2,64,128]{3,2,1,0:T(8,128)S(1)}, u32[]{:S(2)}, u32[]{:S(2)}) collective-permute-start(f32[2,2,64,128]{3,2,1,0:T(8,128)S(1)} %constant_dynamic-update-slice_fusion.25), channel_id=1, source_target_pairs={{31,0},{0,1},{1,2},{2,3},{3,4},{4,5},{5,6},{6,7},{7,8},{8,9},{9,10... | collective-permute-start | bytes 393224 | tf_op jit(solution)/shard_map/while/body/eval_jaxpr/ppermute | solution.py:14
  1578.0 30.8 %collective-permute-start.1 = (bf16[2,128,128]{2,1,0:T(8,128)(2,1)S(1)}, bf16[2,128,128]{2,1,0:T(8,128)(2,1)S(1)}, u32[]{:S(2)}, u32[]{:S(2)}) collective-permute-start(bf16[2,128,128]{2,1,0:T(8,128)(2,1)S(1)} %copy.189), channel_id=1, source_target_pairs={{31,0},{0,1},{1,2},{2,3},{3,4},{4,5},{5,6},{6,7},{7,8},{8,9},{9,10... | collective-permute-start | bytes 196616 | tf_op jit(solution)/shard_map/while/body/eval_jaxpr/ppermute | solution.py:14
  1652.3 32.0 %collective-permute-start.2 = (f32[2,2,64,128]{3,2,1,0:T(8,128)S(1)}, f32[2,2,64,128]{3,2,1,0:T(8,128)S(1)}, u32[]{:S(2)}, u32[]{:S(2)}) collective-permute-start(f32[2,2,64,128]{3,2,1,0:T(8,128)S(1)} %constant_dynamic-update-slice_fusion.25), channel_id=1, source_target_pairs={{31,0},{0,1},{1,2},{2,3},{3,4},{4,5},{5,6},{6,7},{7,8},{8,9},{9,10... | collective-permute-start | bytes 393224 | tf_op jit(solution)/shard_map/while/body/eval_jaxpr/ppermute | solution.py:14
  1654.2 31.5 %collective-permute-start.1 = (bf16[2,128,128]{2,1,0:T(8,128)(2,1)S(1)}, bf16[2,128,128]{2,1,0:T(8,128)(2,1)S(1)}, u32[]{:S(2)}, u32[]{:S(2)}) collective-permute-start(bf16[2,128,128]{2,1,0:T(8,128)(2,1)S(1)} %copy.189), channel_id=1, source_target_pairs={{31,0},{0,1},{1,2},{2,3},{3,4},{4,5},{5,6},{6,7},{7,8},{8,9},{9,10... | collective-permute-start | bytes 196616 | tf_op jit(solution)/shard_map/while/body/eval_jaxpr/ppermute | solution.py:14
  (70 other events, 1887.7 us)
where the time goes:
time: 2030 us; the launch traced here: 1990 us
  waiting for transfers between devices  1040 us (51%)
  blocking collectives  190 us (9%)
  starting transfers between devices  186 us (9%)
  local copies, waits for them, and re-layouts  166 us (8%)
  matrix products  163 us (8%)
  other arithmetic  141 us (7%)
  loops' own time  96.2 us (5%)
    ppermute x96, waiting for transfers between devices, from_behind(): return lax.ppermute(block, axis, route)  1040 us
    psum x1, blocking collectives, per_device(): lax.psum(local_sums, ('outer', 'inner')) / math.sqrt(pair_tokens)  190 us
    ppermute x96, starting transfers between devices, from_behind(): return lax.ppermute(block, axis, route)  186 us
    and x104, other arithmetic, visible(): (k_pos[None, :] >= pair_start) & (k_pos[None, :] < second_start)  125 us
    scatter x256, local copies, waits for them, and re-layouts, backward_tile(): key_grads = key_grads.at[0, k_part].set(k_new).at[1, k_part].set(v_new)  77.1 us
    dot_general x52, matrix products, forward_update(): jnp.einsum('hqk,kd->qhd', weights, v_block.astype(jnp.float32), preferred...  51.2 us
    dot_general x52, matrix products, forward_update(): jnp.einsum('qhd,kd->hqk', q_block, k_block, preferred_element_type=jnp.fl...  50.8 us
    another operation x1, loops' own time, per_device(): lax.fori_loop(0, cycle_size, back_hop, (key_vals, zero_grads, (zero_query...  47.1 us
  transfers between devices with their start and end apart: 96, of which 96 were waited for; matrix products, arithmetic and copies ran while one was open for 10% of the time, Pallas kernels for 0%

commit v1 on v0

v1 whole, which is shorter than its diff:
```python
import functools
import math

import jax
import jax.numpy as jnp
from jax import lax
from jax.experimental import pallas as pl
from jax.experimental.pallas import tpu as pltpu
from jax.sharding import PartitionSpec as P

MESH = pl.DeviceIdType.MESH
BF = jnp.bfloat16
F32 = jnp.float32
HEADS = 8
DH = 128
TOK = 128
HALF = 64
ROWS = HEADS * TOK
UNIT = 4 * TOK
SCALE = 1.0 / math.sqrt(DH)
LOG2E_SCALE = math.log2(math.e) / math.sqrt(DH)
MASKED = -(2.0**99)


class Place:
    def __init__(self):
        outer = lax.axis_index("outer")
        inner = lax.axis_index("inner")
        self.inner = inner
        self.core = outer % 2
        self.x = inner // 8
        self.y = inner % 4
        self.z = (inner // 4) % 2 * 8 + outer // 2
        self.a = self.x + self.core * (self.y - self.x)
        self.b = self.y + self.core * (self.x - self.y)

    def at(self, x, y, z, core):
        return (z % 8 * 2 + core, (x * 2 + z // 8) * 4 + y)

    def near(self, da, db, dz=0):
        a = (self.a + da) % 4
        b = (self.b + db) % 4
        x = a + self.core * (b - a)
        y = b + self.core * (a - b)
        return self.at(x, y, (self.z + dz) % 16, self.core)

    def in_plane(self, slot):
        return self.at(slot // 4, slot % 4, self.z, self.core)

    def along_z(self, z):
        return self.at(self.x, self.y, z, self.core)

    def other_core(self):
        return self.at(self.x, self.y, self.z, 1 - self.core)


def remote(src, dst, send_sem, recv_sem, device):
    return pltpu.make_async_remote_copy(
        src_ref=src,
        dst_ref=dst,
        send_sem=send_sem,
        recv_sem=recv_sem,
        device_id=device,
        device_id_type=MESH,
    )


def kernel(
    q_hbm, k_ref, v_ref, g_hbm, w_ref, bounds_ref, order_ref,
    dq_ref, dk_ref, dv_ref, bias_ref,
    q_in, g_in, kv, feat, qt, gt, q_rows, g_rows, kt, diag,
    e_all, dp_all, m_all, m_run, l_run, d_run, dq_t,
    part, got_b, line, got_a, fin, got_z, sum_kv,
    own_sum, plane_sums, plane_sum, z_sums, z_sum, core_sums,
    in_sem, gather_send, gather_recv, b_send, b_recv, a_send, a_recv, z_sem,
    plane_send, plane_recv, zs_send, zs_recv, core_sem,
):
    me = Place()
    slot = me.x * 4 + me.y
    q_copy = pltpu.make_async_copy(q_hbm.at[0], q_in, in_sem.at[0])
    g_copy = pltpu.make_async_copy(g_hbm.at[0], g_in, in_sem.at[1])
    q_copy.start()
    g_copy.start()

    barrier = pltpu.get_barrier_semaphore()

    def greet(j, carry):
        for device in (me.in_plane((slot + j) % 16), me.along_z((me.z + j) % 16)):
            pl.semaphore_signal(barrier, inc=1, device_id=device, device_id_type=MESH)
        return carry

    lax.fori_loop(1, 16, greet, 0)
    pl.semaphore_signal(barrier, inc=1, device_id=me.other_core(), device_id_type=MESH)
    kv[0, 0, 0, 0] = k_ref[0]
    kv[0, 0, 0, 1] = v_ref[0]
    pl.semaphore_wait(barrier, 31)

    def block(p, s, r, source, device):
        return remote(
            kv.at[source], kv.at[p, s, r], gather_send.at[p, s, r], gather_recv.at[p, s, r], device
        )

    def along_a(p, r):
        return block(p, 0, r, (p, 0, 0), me.near(r, 0))

    def along_b(p, s, r):
        return block(p, s, r, (p, 0, r), me.near(0, s))

    def across():
        return block(1, 0, 0, (0, 0, 0), me.near(0, 0, 8))

    def open_plane(p):
        for r in (2, 1, 3):
            along_a(p, r).start()
        for s in (2, 1, 3):
            along_b(p, s, 0).start()

    def spread_plane(p):
        for r in (1, 3, 2):
            along_a(p, r).wait_recv()
            for s in (2, 1, 3):
                along_b(p, s, r).start()

    across().start()
    open_plane(0)

    pair_start = bounds_ref[0, 0]
    second_start = bounds_ref[0, 1]
    lane = lax.broadcasted_iota(jnp.int32, (TOK, TOK), 1)
    sub = lax.broadcasted_iota(jnp.int32, (TOK, TOK), 0)
    first = order_ref[2 * me.inner]
    second = order_ref[2 * me.inner + 1]
    lane_block = jnp.where(lane < HALF, first, second)
    lane_pos = lane_block * HALF + lane % HALF
    sub_pos = jnp.where(sub < HALF, first, second) * HALF + sub % HALF
    crossing = (sub_pos >= pair_start) & (sub_pos < second_start) & (lane_pos >= second_start)
    allowed = (sub_pos <= lane_pos) & jnp.logical_not(crossing)
    diag[0] = jnp.where(allowed, 0.0, MASKED * LOG2E_SCALE)
    diag[1] = jnp.zeros((TOK, TOK), F32)
    hidden = ((sub < 64) & (sub > lane_block)) | ((sub == 64) & (lane_pos >= second_start))
    q_feat = jnp.where(hidden, MASKED, 0.0).astype(BF)

    half_lane = lax.broadcasted_iota(jnp.int32, (HALF, TOK), 1)
    half_sub = lax.broadcasted_iota(jnp.int32, (HALF, TOK), 0)

    def features(n, carry):
        p, s, r = n // 16, n // 4 % 4, n % 4
        a = (me.a - r + 4) % 4
        b = (me.b - s + 4) % 4
        x = a + me.core * (b - a)
        y = b + me.core * (a - b)
        owner = (x * 2 + (me.z // 8 + p) % 2) * 4 + y
        for h in range(2):
            which = order_ref[2 * owner + h]
            pos = which * HALF + half_sub
            inside = (pos >= pair_start) & (pos < second_start) & (half_lane == 64)
            value = jnp.where((half_lane == which) | inside, 1.0, 0.0).astype(BF)
            feat[p, s, r, h * HALF : (h + 1) * HALF] = value
        return carry

    lax.fori_loop(0, 32, features, 0)
    feat[0, 0, 0] = jnp.zeros((TOK, TOK), BF)

    q_copy.wait()
    g_copy.wait()
    weight = jnp.broadcast_to(w_ref[...].astype(F32) * (1.0 / 16.0), (TOK, TOK)).T
    for h in range(HEADS):
        rows = slice(h * TOK, (h + 1) * TOK)
        q = q_in[:, rows]
        g = (g_in[:, rows].astype(F32) * weight).astype(BF)
        q_rows[rows, :] = q
        g_rows[rows, :] = g
        qt[0:DH, rows] = q.T
        qt[DH : 2 * DH, rows] = q_feat
        gt[:, rows] = g.T
    m_run[...] = jnp.full(m_run.shape, -1e30, F32)
    l_run[...] = jnp.zeros(l_run.shape, F32)
    d_run[...] = jnp.zeros(d_run.shape, F32)
    dq_t[...] = jnp.zeros(dq_t.shape, F32)
    sum_kv[...] = jnp.zeros(sum_kv.shape, F32)

    def first_pass(p, s, own):
        keys = kv[p, s, :, 0].reshape(UNIT, DH)
        vals = kv[p, s, :, 1].reshape(UNIT, DH)
        wide = jnp.concatenate([keys, feat[p, s].reshape(UNIT, DH)], axis=1)
        scores = jnp.dot(wide, qt[...], preferred_element_type=F32) * LOG2E_SCALE
        tri = jnp.concatenate([diag[own]] * HEADS, axis=1)
        scores = jnp.concatenate([scores[0:TOK] + tri, scores[TOK:]], axis=0)
        old = m_run[...]
        new = jnp.maximum(old, jnp.max(scores, axis=0, keepdims=True))
        factor = jnp.exp2(old - new)
        e = jnp.exp2(scores - new)
        dp = jnp.dot(vals, gt[...], preferred_element_type=F32)
        l_run[...] = l_run[...] * factor + jnp.sum(e, axis=0, keepdims=True)
        d_run[...] = d_run[...] * factor + jnp.sum(e * dp, axis=0, keepdims=True)
        e_all[p, s] = e.astype(BF)
        dp_all[p, s] = dp
        m_all[p, s] = new
        m_run[...] = new
        for r in range(4):
            kt[p, s, :, r * TOK : (r + 1) * TOK] = kv[p, s, r, 0].T

    for p in range(2):
        if p == 1:
            across().wait_recv()
            open_plane(1)
        spread_plane(p)

        def first_unit(t, carry, p=p):
            s = t + t // 2 * (5 - 2 * t)

            @pl.when(t > 0)
            def _():
                for r in (0, 1, 3, 2):
                    along_b(p, s, r).wait_recv()

            first_pass(p, s, 1 if p == 1 else jnp.minimum(t, 1))
            return carry

        lax.fori_loop(0, 4, first_unit, 0)

    inverse = 1.0 / l_run[...]
    d_run[...] = d_run[...] * inverse
    l_run[...] = inverse

    def second_pass(p, s):
        share = jnp.exp2(m_all[p, s] - m_run[...]) * l_run[...]

        def tile(t, carry):
            rows = pl.ds(pl.multiple_of(t * 256, 256), 256)
            probs = e_all[p, s, rows, :].astype(F32) * share
            probs_low = probs.astype(BF)
            ds = (probs * (dp_all[p, s, rows, :] - d_run[...])).astype(BF)
            dk = jnp.dot(ds, q_rows[...], preferred_element_type=F32) * SCALE
            dv = jnp.dot(probs_low, g_rows[...], preferred_element_type=F32)
            for n in range(2):
                part[p, s, 2 * t + n, 0] = dk[n * TOK : (n + 1) * TOK].astype(BF)
                part[p, s, 2 * t + n, 1] = dv[n * TOK : (n + 1) * TOK].astype(BF)
            sum_kv[0] += jnp.sum(dk.reshape(32, 8, DH), axis=0)
            sum_kv[1] += jnp.sum(dv.reshape(32, 8, DH), axis=0)
            dq_t[...] += jnp.dot(kt[p, s, :, rows], ds, preferred_element_type=F32)
            return carry

        lax.fori_loop(0, 2, tile, 0)

    def back_b(p, s):
        return remote(
            part.at[p, s], got_b.at[p, s - 1], b_send.at[p, s - 1], b_recv.at[p, s - 1],
            me.near(0, 4 - s),
        )

    def back_a(p, r):
        return remote(
            line.at[p, r], got_a.at[p, r - 1], a_send.at[p, r - 1], a_recv.at[p, r - 1],
            me.near(4 - r, 0),
        )

    def back_z():
        return remote(fin, got_z, z_sem.at[0], z_sem.at[1], me.near(0, 0, 8))

    def second_unit(p):
        def unit(t, carry):
            s = 3 - t
            second_pass(p, s)

            @pl.when(s > 0)
            def _():
                back_b(p, s).start()

            return carry

        return unit

    def add_b(p):
        for s in (1, 2, 3):
            back_b(p, s).wait_recv()
        for r in (2, 1, 3, 0):
            total = part[p, 0, r].astype(F32)
            for s in range(3):
                total = total + got_b[p, s, r].astype(F32)
            line[p, r] = total.astype(BF)
            if r > 0:
                back_a(p, r).start()

    def add_a(p):
        total = line[p, 0].astype(F32)
        for r in (1, 3, 2):
            back_a(p, r).wait_recv()
            total = total + got_a[p, r - 1].astype(F32)
        return total

    lax.fori_loop(0, 4, second_unit(1), 0)
    lax.fori_loop(0, 2, second_unit(0), 0)
    add_b(1)
    lax.fori_loop(2, 3, second_unit(0), 0)
    fin[...] = add_a(1).astype(BF)
    back_z().start()
    lax.fori_loop(3, 4, second_unit(0), 0)

    own_sum[...] = jnp.zeros(own_sum.shape, F32)
    for h in range(HEADS):
        rows = slice(h * TOK, (h + 1) * TOK)
        dq = dq_t[:, rows].T * SCALE
        dq_ref[0, :, rows] = dq.astype(BF)
        own_sum[h : h + 1, :] = jnp.sum(dq, axis=0, keepdims=True)
    own_sum[8:9, :] = jnp.sum(sum_kv[0], axis=0, keepdims=True)
    own_sum[9:10, :] = jnp.sum(sum_kv[1], axis=0, keepdims=True)

    def plane_copy(j):
        return remote(
            own_sum, plane_sums.at[slot], plane_send.at[j], plane_recv.at[slot],
            me.in_plane((slot + j) % 16),
        )

    def plane_arrival(j):
        there = (slot + j) % 16
        return remote(
            own_sum, plane_sums.at[there], plane_send.at[j], plane_recv.at[there],
            me.in_plane(there),
        )

    def z_copy(j):
        return remote(
            plane_sum, z_sums.at[me.z], zs_send.at[j], zs_recv.at[me.z],
            me.along_z((me.z + j) % 16),
        )

    def z_arrival(j):
        there = (me.z + j) % 16
        return remote(
            plane_sum, z_sums.at[there], zs_send.at[j], zs_recv.at[there], me.along_z(there)
        )

    def core_copy():
        return remote(
            z_sum, core_sums.at[me.core], core_sem.at[0], core_sem.at[1], me.other_core()
        )

    def each(action):
        def step(j, carry):
            action(j)
            return carry

        lax.fori_loop(1, 16, step, 0)

    def added(ref, count):
        total = ref[0]
        for n in range(1, count):
            total = total + ref[n]
        return total

    each(lambda j: plane_copy(j).start())
    plane_sums[slot] = own_sum[...]
    add_b(0)
    each(lambda j: plane_arrival(j).wait_recv())
    plane_sum[...] = added(plane_sums, 16)
    each(lambda j: z_copy(j).start())
    z_sums[me.z] = plane_sum[...]
    total = add_a(0)
    dk_ref[0] = total[0].astype(BF)
    dv_ref[0] = total[1].astype(BF)
    back_z().wait_recv()
    dk_ref[0] = (total[0] + got_z[0].astype(F32)).astype(BF)
    dv_ref[0] = (total[1] + got_z[1].astype(F32)).astype(BF)
    each(lambda j: z_arrival(j).wait_recv())
    z_sum[...] = added(z_sums, 16)
    core_copy().start()
    core_sums[me.core] = z_sum[...]
    remote(
        z_sum, core_sums.at[1 - me.core], core_sem.at[0], core_sem.at[1], me.other_core()
    ).wait_recv()
    bias_ref[...] = added(core_sums, 2) * (1.0 / 256.0)

    across().wait_send()
    for p in range(2):
        for r in (1, 2, 3):
            along_a(p, r).wait_send()
            back_a(p, r).wait_send()
            back_b(p, r).wait_send()
            for s in range(4):
                along_b(p, r, s).wait_send()
    back_z().wait_send()
    each(lambda j: plane_copy(j).wait_send())
    each(lambda j: z_copy(j).wait_send())
    core_copy().wait_send()


def per_device(q_heads, k_head, v_head, out_grad, weight_codes, bounds, block_order):
    vmem = pl.BlockSpec(memory_space=pltpu.VMEM)
    smem = pl.BlockSpec(memory_space=pltpu.SMEM)
    hbm = pl.BlockSpec(memory_space=pl.ANY)
    low = lambda *shape: pltpu.VMEM(shape, BF)
    full = lambda *shape: pltpu.VMEM(shape, F32)
    dma = lambda *shape: pltpu.SemaphoreType.DMA(shape)
    scratch = [
        low(TOK, ROWS), low(TOK, ROWS),
        low(2, 4, 4, 2, TOK, DH), low(2, 4, 4, TOK, DH),
        low(2 * DH, ROWS), low(DH, ROWS), low(ROWS, DH), low(ROWS, DH),
        low(2, 4, DH, UNIT), full(2, TOK, TOK),
        low(2, 4, UNIT, ROWS), full(2, 4, UNIT, ROWS), full(2, 4, 1, ROWS),
        full(1, ROWS), full(1, ROWS), full(1, ROWS), full(DH, ROWS),
        low(2, 4, 4, 2, TOK, DH), low(2, 3, 4, 2, TOK, DH), low(2, 4, 2, TOK, DH),
        low(2, 3, 2, TOK, DH), low(2, TOK, DH), low(2, TOK, DH), full(2, 8, DH),
        full(16, DH), full(16, 16, DH), full(16, DH), full(16, 16, DH), full(16, DH),
        full(2, 16, DH),
        dma(2), dma(2, 4, 4), dma(2, 4, 4), dma(2, 3), dma(2, 3), dma(2, 3), dma(2, 3), dma(2),
        dma(16), dma(16), dma(16), dma(16), dma(2),
    ]
    dq, dk, dv, bias = pl.pallas_call(
        kernel,
        out_shape=(
            jax.ShapeDtypeStruct((1, TOK, ROWS), BF),
            jax.ShapeDtypeStruct((1, TOK, DH), BF),
            jax.ShapeDtypeStruct((1, TOK, DH), BF),
            jax.ShapeDtypeStruct((16, DH), F32),
        ),
        in_specs=[hbm, vmem, vmem, hbm, vmem, smem, smem],
        out_specs=(vmem, vmem, vmem, vmem),
        scratch_shapes=scratch,
        compiler_params=pltpu.CompilerParams(
            collective_id=0, has_side_effects=True, vmem_limit_bytes=56 * 2**20
        ),
    )(q_heads, k_head, v_head, out_grad, weight_codes, bounds, block_order)
    return dq, dk, dv, bias[:10].reshape(1280)


def solution(mesh):
    return jax.shard_map(
        per_device,
        mesh=mesh,
        in_specs=(
            P("outer", "inner", None),
            P("outer", "inner", None),
            P("outer", "inner", None),
            P("outer", "inner", None),
            P("outer", "inner"),
            P("outer", None),
            P(),
        ),
        out_specs=(
            P("outer", "inner", None),
            P("outer", "inner", None),
            P("outer", "inner", None),
            P(),
        ),
        check_vma=False,
    )
```

time: 2030 us -> 87.7 us (0.04); the launches traced: 1990 us -> 87.4 us
  waiting for transfers between devices: 1040 us -> 0 us
  blocking collectives: 190 us -> 0 us
  starting transfers between devices: 186 us -> 0 us
  matrix products: 163 us -> 0 us
  local copies, waits for them, and re-layouts: 166 us -> 4.36 us
  other arithmetic: 141 us -> 0 us
  loops' own time: 96.2 us -> 0 us
  Pallas kernels: 0 us -> 82.4 us
    ppermute x96 -> x0, waiting for transfers between devices: 1040 us -> none  [from_behind(): return lax.ppermute(block, axis, route)]
    psum x1 -> x0, blocking collectives: 190 us -> none  [per_device(): lax.psum(local_sums, ('outer', 'inner')) / math.sqrt(pair_tokens)]
    ppermute x96 -> x0, starting transfers between devices: 186 us -> none  [from_behind(): return lax.ppermute(block, axis, route)]
    dot_general x364 -> x0, matrix products: 163 us -> none  [the longest x52 51.2 us: forward_update(): jnp.einsum('hqk,kd->qhd', weights, v_block.astype(jnp.float32), preferred...]
    and x208 -> x0, other arithmetic: 134 us -> none  [the longest x104 125 us: visible(): (k_pos[None, :] >= pair_start) & (k_pos[None, :] < second_start)]
    another operation x258 -> x0, loops' own time: 96.2 us -> none  [the longest x1 47.1 us: per_device(): lax.fori_loop(0, cycle_size, back_hop, (key_vals, zero_grads, (zero_query...]
    pallas_call x0 -> x1, Pallas kernels: none -> 82.4 us  [per_device(): pl.pallas_call(kernel, out_shape=(jax.ShapeDtypeStruct((1, TOK, ROWS), BF...]
    scatter x256 -> x0, local copies, waits for them, and re-layouts: 77.1 us -> none  [backward_tile(): key_grads = key_grads.at[0, k_part].set(k_new).at[1, k_part].set(v_new)]
  transfers between devices with their start and end apart: 96 -> 0, of which waited for: 96 -> 0; matrix products, arithmetic and copies ran while one was open for 10% -> 0% of each run, Pallas kernels for 0% -> 0%
where the time goes in v1:
time: 87.7 us; the launch traced here: 87.4 us
  Pallas kernels  82.4 us (94%)
  local copies, waits for them, and re-layouts  4.36 us (5%)
    pallas_call x1, Pallas kernels, per_device(): pl.pallas_call(kernel, out_shape=(jax.ShapeDtypeStruct((1, TOK, ROWS), BF...  82.4 us
    unnamed x7, local copies, waits for them, and re-layouts  3.06 us

profile of v1, /device:TPU:1, one launch (start us, length us, event | category | flops | bytes accessed | tf_op | source)
XLA Modules:
  0.0 87.4 jit_solution(11052086489278380197)
XLA Ops:
  0.6 82.4 %shard_map.102 = (bf16[1,128,1024]{2,1,0:T(8,128)(2,1)}, bf16[1,128,128]{2,1,0:T(8,128)(2,1)}, bf16[1,128,128]{2,1,0:T(8,128)(2,1)}, f32[16,128]{1,0:T(8,128)}) custom-call(bf16[1,128,1024]{2,1,0:T(8,128)(2,1)} %q_hbm.1, bf16[1,128,128]{2,1,0:T(8,128)(2,1)} %k_ref.1, bf16[1,128,128]{2,1,0:T(8,128)(2,1)} %v_ref.1, bf16[1,128,1024]{2,1,0:T(8,128)(2,1)} %g_hbm.1, ...), custom_call_target="tpu_custom_call" | custom-call | tf_op jit(solution)/shard_map/pallas_call | solution.py:409
  83.1 1.3 %slice_bitcast_fusion = f32[1280]{0:T(1024)} fusion(f32[16,128]{1,0:T(8,128)} %get-tuple-element.11), kind=kLoop, calls=%fused_computation | loop fusion | bytes 10240 | tf_op jit(solution)/shard_map/reshape | solution.py:424
  84.3 0.0 copy-start.1
  84.4 1.7 %copy.14 = bf16[1,128,1024]{2,1,0:T(8,128)(2,1)} copy(bf16[1,128,1024]{2,1,0:T(8,128)(2,1)} %get-tuple-element.16) | data formatting | bytes 524288
  86.0 0.0 copy-done.1
  86.0 0.0 copy-start
  86.0 0.6 copy.15
  86.6 0.2 copy-done
  86.8 0.6 copy.16
Async XLA Ops:
  84.3 1.7 %copy-start.1 = (bf16[1,128,128]{2,1,0:T(8,128)(2,1)S(1)}, bf16[1,128,128]{2,1,0:T(8,128)(2,1)}, u32[]{:S(2)}) copy-start(bf16[1,128,128]{2,1,0:T(8,128)(2,1)} %get-tuple-element.17) | copy-start | bytes 98308
  86.0 0.8 copy-start

commit v2 on v1

v2 whole, which is shorter than its diff:
```python
import functools
import math

import jax
import jax.numpy as jnp
from jax import lax
from jax.experimental import pallas as pl
from jax.experimental.pallas import tpu as pltpu
from jax.sharding import PartitionSpec as P

MESH = pl.DeviceIdType.MESH
BF = jnp.bfloat16
F32 = jnp.float32
HEADS = 8
DH = 128
TOK = 128
HALF = 64
ROWS = HEADS * TOK
UNIT = 4 * TOK
SCALE = 1.0 / math.sqrt(DH)
LOG2E_SCALE = math.log2(math.e) / math.sqrt(DH)
MASKED = -(2.0**99)


class Place:
    def __init__(self):
        outer = lax.axis_index("outer")
        inner = lax.axis_index("inner")
        self.inner = inner
        self.core = outer % 2
        self.x = inner // 8
        self.y = inner % 4
        self.z = (inner // 4) % 2 * 8 + outer // 2
        self.a = self.x + self.core * (self.y - self.x)
        self.b = self.y + self.core * (self.x - self.y)

    def at(self, x, y, z, core):
        return (z % 8 * 2 + core, (x * 2 + z // 8) * 4 + y)

    def near(self, da, db, dz=0):
        a = (self.a + da) % 4
        b = (self.b + db) % 4
        x = a + self.core * (b - a)
        y = b + self.core * (a - b)
        return self.at(x, y, (self.z + dz) % 16, self.core)

    def in_plane(self, slot, core):
        return self.at(slot // 4, slot % 4, self.z, core)

    def along_z(self, z):
        return self.at(self.x, self.y, z, self.core)


def remote(src, dst, send_sem, recv_sem, device):
    return pltpu.make_async_remote_copy(
        src_ref=src,
        dst_ref=dst,
        send_sem=send_sem,
        recv_sem=recv_sem,
        device_id=device,
        device_id_type=MESH,
    )


def kernel(
    q_hbm, k_hbm, v_hbm, g_hbm, w_hbm, bounds_hbm, order_hbm,
    dq_ref, dk_ref, dv_ref, bias_ref,
    q_in, k_in, v_in, g_in, w_in, bounds_ref, order_ref,
    kv, feat, q_wide, q_t, g_rows, g_t, keys, diag,
    e_all, dp_all, m_all, m_run, l_run, d_run, dq_all,
    part, got_b, line, got_a, fin, got_z, sum_kv, dq_out, kv_total, kv_out,
    own_sum, plane_rows, row_sum, z_rows, all_rows,
    in_sem, out_sem, gather_send, gather_recv, b_send, b_recv, a_send, a_recv, z_sem,
    plane_send, plane_recv, zs_send, zs_recv, last_send, last_recv,
):
    me = Place()
    slot = me.x * 4 + me.y
    arrays = (
        (k_hbm.at[0], k_in), (v_hbm.at[0], v_in), (bounds_hbm, bounds_ref),
        (order_hbm, order_ref), (w_hbm, w_in), (q_hbm.at[0], q_in), (g_hbm.at[0], g_in),
    )
    loads = [
        pltpu.make_async_copy(source, target, in_sem.at[n])
        for n, (source, target) in enumerate(arrays)
    ]
    for load in loads:
        load.start()

    barrier = pltpu.get_barrier_semaphore()

    def greet(j, carry):
        there = (slot + j) % 16
        for device in (
            me.along_z((me.z + j) % 16), me.in_plane(there, me.core), me.in_plane(there, 1 - me.core)
        ):
            pl.semaphore_signal(barrier, inc=1, device_id=device, device_id_type=MESH)
        return carry

    pl.semaphore_signal(
        barrier, inc=1, device_id=me.in_plane(slot, 1 - me.core), device_id_type=MESH
    )
    lax.fori_loop(1, 16, greet, 0)
    for load in loads[:4]:
        load.wait()
    kv[0, 0, 0, 0] = k_in[...].T
    kv[0, 0, 0, 1] = v_in[...].T

    pair_start = bounds_ref[0, 0]
    second_start = bounds_ref[0, 1]
    lane = lax.broadcasted_iota(jnp.int32, (TOK, TOK), 1)
    sub = lax.broadcasted_iota(jnp.int32, (TOK, TOK), 0)
    first = order_ref[2 * me.inner]
    second = order_ref[2 * me.inner + 1]
    sub_block = jnp.where(sub < HALF, first, second)
    sub_pos = sub_block * HALF + sub % HALF
    lane_pos = jnp.where(lane < HALF, first, second) * HALF + lane % HALF
    crossing = (lane_pos >= pair_start) & (lane_pos < second_start) & (sub_pos >= second_start)
    allowed = (lane_pos <= sub_pos) & jnp.logical_not(crossing)
    diag[0] = jnp.where(allowed, 0.0, MASKED * LOG2E_SCALE)
    diag[1] = jnp.zeros((TOK, TOK), F32)
    hidden = ((lane < 64) & (lane > sub_block)) | ((lane == 64) & (sub_pos >= second_start))
    q_feat = jnp.where(hidden, MASKED, 0.0).astype(BF)

    def features(n, carry):
        p, s, r = n // 16, n // 4 % 4, n % 4
        a = (me.a - r + 4) % 4
        b = (me.b - s + 4) % 4
        x = a + me.core * (b - a)
        y = b + me.core * (a - b)
        owner = (x * 2 + (me.z // 8 + p) % 2) * 4 + y
        which = jnp.where(lane < HALF, order_ref[2 * owner], order_ref[2 * owner + 1])
        pos = which * HALF + lane % HALF
        inside = (pos >= pair_start) & (pos < second_start) & (sub == 64)
        feat[p, s, r] = jnp.where((sub == which) | inside, 1.0, 0.0).astype(BF)
        return carry

    lax.fori_loop(0, 32, features, 0)
    feat[0, 0, 0] = jnp.zeros((TOK, TOK), BF)

    pl.semaphore_wait(barrier, 46)

    def block(p, s, r, source, device):
        return remote(
            kv.at[source], kv.at[p, s, r], gather_send.at[p, s, r], gather_recv.at[p, s, r], device
        )

    def along_a(p, r):
        return block(p, 0, r, (p, 0, 0), me.near(r, 0))

    def along_b(p, s, r):
        return block(p, s, r, (p, 0, r), me.near(0, s))

    def across():
        return block(1, 0, 0, (0, 0, 0), me.near(0, 0, 8))

    def open_plane(p):
        for r in (2, 1, 3):
            along_a(p, r).start()
        for s in (2, 1, 3):
            along_b(p, s, 0).start()

    def pass_on(p, r):
        along_a(p, r).wait_recv()
        for s in (2, 1, 3):
            along_b(p, s, r).start()

    across().start()
    open_plane(0)

    for load in loads[4:]:
        load.wait()
    weight = jnp.broadcast_to(w_in[...].astype(F32) * (1.0 / 16.0), (TOK, TOK)).T
    for h in range(HEADS):
        rows = slice(h * TOK, (h + 1) * TOK)
        q = q_in[:, rows]
        g = (g_in[:, rows].astype(F32) * weight).astype(BF)
        q_wide[rows, 0:DH] = q
        q_wide[rows, DH : 2 * DH] = q_feat
        q_t[:, rows] = q.T
        g_rows[rows, :] = g
        g_t[:, rows] = g.T
    m_run[...] = jnp.full(m_run.shape, -1e30, F32)
    l_run[...] = jnp.zeros(l_run.shape, F32)
    d_run[...] = jnp.zeros(d_run.shape, F32)
    dq_all[...] = jnp.zeros(dq_all.shape, F32)
    sum_kv[...] = jnp.zeros(sum_kv.shape, F32)

    def first_pass(p, s, own):
        wide = jnp.concatenate(
            [
                jnp.concatenate([kv[p, s, r, 0] for r in range(4)], axis=1),
                jnp.concatenate([feat[p, s, r] for r in range(4)], axis=1),
            ],
            axis=0,
        )
        scores = jnp.dot(q_wide[...], wide, preferred_element_type=F32) * LOG2E_SCALE
        vals = jnp.concatenate([kv[p, s, r, 1] for r in range(4)], axis=1)
        dp = jnp.dot(g_rows[...], vals, preferred_element_type=F32)
        tri = jnp.concatenate([diag[own]] * HEADS, axis=0)
        blocks = [scores[:, r * TOK : (r + 1) * TOK] for r in range(4)]
        blocks[0] = blocks[0] + tri
        old = m_run[...]
        new = old
        for r in range(4):
            new = jnp.maximum(new, blocks[r])
        factor = jnp.exp2(old - new)
        l_new = l_run[...] * factor
        d_new = d_run[...] * factor
        for r in range(4):
            e = jnp.exp2(blocks[r] - new)
            dp_r = dp[:, r * TOK : (r + 1) * TOK]
            l_new = l_new + e
            d_new = d_new + e * dp_r
            e_all[p, s, r] = e.astype(BF)
            dp_all[p, s, r] = dp_r
        l_run[...] = l_new
        d_run[...] = d_new
        m_all[p, s] = new
        m_run[...] = new
        for r in range(4):
            keys[p, s, r * TOK : (r + 1) * TOK, :] = kv[p, s, r, 0].T

    for r in (1, 3, 2):
        pass_on(0, r)

    def first_unit(p):
        def unit(t, carry):
            s = t + t // 2 * (5 - 2 * t)

            @pl.when(t > 0)
            def _():
                if p == 0:
                    pass_on(1, s)
                for r in (0, 1, 3, 2):
                    along_b(p, s, r).wait_recv()

            first_pass(p, s, 1 if p == 1 else jnp.minimum(t, 1))

            if p == 0:

                @pl.when(t == 0)
                def _():
                    across().wait_recv()
                    open_plane(1)

            return carry

        return unit

    lax.fori_loop(0, 4, first_unit(0), 0)
    lax.fori_loop(0, 4, first_unit(1), 0)

    top = jnp.max(m_run[...], axis=1, keepdims=True)
    factor = jnp.exp2(m_run[...] - top)
    inverse = 1.0 / jnp.sum(l_run[...] * factor, axis=1, keepdims=True)
    delta = jnp.sum(d_run[...] * factor, axis=1, keepdims=True) * inverse
    m_run[...] = jnp.broadcast_to(top, m_run.shape)
    l_run[...] = jnp.broadcast_to(inverse, l_run.shape)
    d_run[...] = jnp.broadcast_to(delta, d_run.shape)

    def second_pass(p, s, with_v, with_k):
        share = jnp.exp2(m_all[p, s] - m_run[...]) * l_run[...]
        for t in range(2):
            low = []
            ds = []
            for r in (2 * t, 2 * t + 1):
                probs = e_all[p, s, r].astype(F32) * share
                if with_v:
                    low.append(probs.astype(BF))
                if with_k:
                    ds.append((probs * (dp_all[p, s, r] - d_run[...])).astype(BF))
            if with_v:
                dv = jnp.dot(g_t[...], jnp.concatenate(low, axis=1), preferred_element_type=F32)
                for n in range(2):
                    part[p, s, 1, 2 * t + n] = dv[:, n * TOK : (n + 1) * TOK].astype(BF)
                sum_kv[1] += dv[:, :TOK] + dv[:, TOK:]
            if with_k:
                ds = jnp.concatenate(ds, axis=1)
                dk = jnp.dot(q_t[...], ds, preferred_element_type=F32) * SCALE
                for n in range(2):
                    part[p, s, 0, 2 * t + n] = dk[:, n * TOK : (n + 1) * TOK].astype(BF)
                sum_kv[0] += dk[:, :TOK] + dk[:, TOK:]
                dq_all[...] += jnp.dot(
                    ds, keys[p, s, 256 * t : 256 * t + 256, :], preferred_element_type=F32
                )

    def back_b(p, s, v):
        return remote(
            part.at[p, s, v], got_b.at[p, s - 1, v], b_send.at[p, s - 1, v],
            b_recv.at[p, s - 1, v], me.near(0, 4 - s),
        )

    def back_a(p, r, v):
        return remote(
            line.at[p, r, v], got_a.at[p, r - 1, v], a_send.at[p, r - 1, v],
            a_recv.at[p, r - 1, v], me.near(4 - r, 0),
        )

    def back_z(v):
        return remote(fin.at[v], got_z.at[v], z_sem.at[v, 0], z_sem.at[v, 1], me.near(0, 0, 8))

    def far_unit(v):
        def unit(t, carry):
            s = 3 - t
            second_pass(1, s, v == 1, v == 0)

            @pl.when(s > 0)
            def _():
                back_b(1, s, v).start()

            return carry

        return unit

    def near_unit(t, carry):
        second_pass(0, 3 - t, True, True)
        return carry

    def add_b(p, v):
        for s in (3, 2, 1):
            back_b(p, s, v).wait_recv()
        for r in (2, 1, 3, 0):
            total = part[p, 0, v, r].astype(F32)
            for s in range(3):
                total = total + got_b[p, s, v, r].astype(F32)
            line[p, r, v] = total.astype(BF)
            if r > 0:
                back_a(p, r, v).start()

    def add_a(p, v):
        total = line[p, 0, v].astype(F32)
        for r in (1, 3, 2):
            back_a(p, r, v).wait_recv()
            total = total + got_a[p, r - 1, v].astype(F32)
        return total

    lax.fori_loop(0, 4, far_unit(1), 0)
    lax.fori_loop(0, 4, far_unit(0), 0)
    lax.fori_loop(0, 2, near_unit, 0)
    add_b(1, 1)
    back_b(0, 2, 1).start()
    back_b(0, 2, 0).start()
    lax.fori_loop(2, 4, near_unit, 0)

    for h in range(HEADS):
        rows = slice(h * TOK, (h + 1) * TOK)
        dq = dq_all[rows, :] * SCALE
        dq_out[:, rows] = dq.astype(BF)
        own_sum[h] = jnp.sum(dq, axis=0, keepdims=True)
    own_sum[8] = jnp.sum(sum_kv[0].T, axis=0, keepdims=True)
    own_sum[9] = jnp.sum(sum_kv[1].T, axis=0, keepdims=True)
    number = me.core * 16 + slot
    adds = (slot < 10) & (me.core == slot % 2)

    def plane_copy(j):
        return remote(
            own_sum.at[j], plane_rows.at[number], plane_send.at[j], plane_recv.at[number],
            me.in_plane(j, j % 2),
        )

    def plane_arrival(j):
        there = (number + j) % 32
        return remote(
            own_sum.at[0], plane_rows.at[there], plane_send.at[0], plane_recv.at[there],
            me.in_plane(there % 16, there // 16),
        )

    def z_copy(j):
        return remote(
            row_sum, z_rows.at[me.z], zs_send.at[j], zs_recv.at[me.z],
            me.along_z((me.z + j) % 16),
        )

    def z_arrival(j):
        there = (me.z + j) % 16
        return remote(
            row_sum, z_rows.at[there], zs_send.at[j], zs_recv.at[there], me.along_z(there)
        )

    def last_copy(j):
        there = (number + j) % 32
        return remote(
            all_rows.at[slot], all_rows.at[slot], last_send.at[j], last_recv.at[slot],
            me.in_plane(there % 16, there // 16),
        )

    def last_arrival(j):
        return remote(
            all_rows.at[j], all_rows.at[j], last_send.at[0], last_recv.at[j],
            me.in_plane(j, j % 2),
        )

    def each(start, stop, action):
        def step(j, carry):
            action(j)
            return carry

        lax.fori_loop(start, stop, step, 0)

    def each_row(action):
        def unless_mine(j):
            @pl.when(jnp.logical_not((slot == j) & (me.core == j % 2)))
            def _():
                action(j)

        each(0, 10, unless_mine)

    def added(ref, count):
        total = ref[0]
        for n in range(1, count):
            total = total + ref[n]
        return total

    each_row(lambda j: plane_copy(j).start())
    add_b(1, 0)
    for v in (1, 0):
        back_b(0, 1, v).start()
        back_b(0, 3, v).start()
    fin[1] = add_a(1, 1).astype(BF)
    back_z(1).start()
    dq_copy = pltpu.make_async_copy(dq_out, dq_ref.at[0], out_sem.at[0])
    dq_copy.start()

    @pl.when(adds)
    def _():
        plane_rows[number] = own_sum[slot]
        each(1, 32, lambda j: plane_arrival(j).wait_recv())
        row_sum[...] = added(plane_rows, 32)
        each(1, 16, lambda j: z_copy(j).start())
        z_rows[me.z] = row_sum[...]

    fin[0] = add_a(1, 0).astype(BF)
    back_z(0).start()
    add_b(0, 1)
    add_b(0, 0)

    @pl.when(adds)
    def _():
        each(1, 16, lambda j: z_arrival(j).wait_recv())
        all_rows[slot] = added(z_rows, 16) * (1.0 / 256.0)
        each(1, 32, lambda j: last_copy(j).start())

    kv_total[1] = add_a(0, 1)
    kv_total[0] = add_a(0, 0)
    for v in (1, 0):
        back_z(v).wait_recv()
        kv_out[v] = (kv_total[v] + got_z[v].astype(F32)).T.astype(BF)
    dk_copy = pltpu.make_async_copy(kv_out.at[0], dk_ref.at[0], out_sem.at[1])
    dv_copy = pltpu.make_async_copy(kv_out.at[1], dv_ref.at[0], out_sem.at[2])
    dk_copy.start()
    dv_copy.start()
    each_row(lambda j: last_arrival(j).wait_recv())
    for n in range(10):
        bias_ref[n] = all_rows[n]
    dq_copy.wait()
    dk_copy.wait()
    dv_copy.wait()

    across().wait_send()
    for p in range(2):
        for r in (1, 2, 3):
            along_a(p, r).wait_send()
            for v in range(2):
                back_a(p, r, v).wait_send()
                back_b(p, r, v).wait_send()
            for s in range(4):
                along_b(p, r, s).wait_send()
    for v in range(2):
        back_z(v).wait_send()
    each_row(lambda j: plane_copy(j).wait_send())

    @pl.when(adds)
    def _():
        each(1, 16, lambda j: z_copy(j).wait_send())
        each(1, 32, lambda j: last_copy(j).wait_send())


def deliver(dq_in, dk_in, dv_in, bias_in, dq_ref, dk_ref, dv_ref, bias_ref):
    dq_ref[...] = dq_in[...]
    dk_ref[...] = dk_in[...]
    dv_ref[...] = dv_in[...]
    for n in range(10):
        bias_ref[n * DH : (n + 1) * DH] = bias_in[n, 0]


def per_device(q_heads, k_head, v_head, out_grad, weight_codes, bounds, block_order):
    vmem = pl.BlockSpec(memory_space=pltpu.VMEM)
    hbm = pl.BlockSpec(memory_space=pl.ANY)
    low = lambda *shape: pltpu.VMEM(shape, BF)
    full = lambda *shape: pltpu.VMEM(shape, F32)
    dma = lambda *shape: pltpu.SemaphoreType.DMA(shape)
    scratch = [
        low(TOK, ROWS), low(TOK, DH), low(TOK, DH), low(TOK, ROWS),
        pltpu.VMEM((1, TOK), jnp.int32), pltpu.SMEM((1, 2), jnp.int32), pltpu.SMEM((64,), jnp.int32),
        low(2, 4, 4, 2, DH, TOK), low(2, 4, 4, TOK, TOK),
        low(ROWS, 2 * DH), low(DH, ROWS), low(ROWS, DH), low(DH, ROWS),
        low(2, 4, UNIT, DH), full(2, TOK, TOK),
        low(2, 4, 4, ROWS, TOK), full(2, 4, 4, ROWS, TOK), full(2, 4, ROWS, TOK),
        full(ROWS, TOK), full(ROWS, TOK), full(ROWS, TOK), full(ROWS, DH),
        low(2, 4, 2, 4, DH, TOK), low(2, 3, 2, 4, DH, TOK), low(2, 4, 2, DH, TOK),
        low(2, 3, 2, DH, TOK), low(2, DH, TOK), low(2, DH, TOK), full(2, DH, TOK),
        low(TOK, ROWS), full(2, DH, TOK), low(2, TOK, DH),
        full(10, 1, DH), full(32, 1, DH), full(1, DH), full(16, 1, DH), full(10, 1, DH),
        dma(7), dma(3), dma(2, 4, 4), dma(2, 4, 4), dma(2, 3, 2), dma(2, 3, 2), dma(2, 3, 2),
        dma(2, 3, 2), dma(2, 2), dma(10), dma(32), dma(16), dma(16), dma(32), dma(10),
    ]
    dq, dk, dv, bias = pl.pallas_call(
        kernel,
        out_shape=(
            jax.ShapeDtypeStruct((1, TOK, ROWS), BF),
            jax.ShapeDtypeStruct((1, TOK, DH), BF),
            jax.ShapeDtypeStruct((1, TOK, DH), BF),
            jax.ShapeDtypeStruct((10, 1, DH), F32),
        ),
        in_specs=[hbm] * 7,
        out_specs=(hbm, hbm, hbm, vmem),
        scratch_shapes=scratch,
        compiler_params=pltpu.CompilerParams(
            collective_id=0, has_side_effects=True, vmem_limit_bytes=56 * 2**20
        ),
    )(q_heads, k_head, v_head, out_grad, weight_codes, bounds, block_order)
    return pl.pallas_call(
        deliver,
        out_shape=(
            jax.ShapeDtypeStruct((1, TOK, ROWS), BF),
            jax.ShapeDtypeStruct((1, TOK, DH), BF),
            jax.ShapeDtypeStruct((1, TOK, DH), BF),
            jax.ShapeDtypeStruct((1280,), F32),
        ),
        in_specs=[vmem] * 4,
        out_specs=(vmem,) * 4,
    )(dq, dk, dv, bias)


def solution(mesh):
    return jax.shard_map(
        per_device,
        mesh=mesh,
        in_specs=(
            P("outer", "inner", None),
            P("outer", "inner", None),
            P("outer", "inner", None),
            P("outer", "inner", None),
            P("outer", "inner"),
            P("outer", None),
            P(),
        ),
        out_specs=(
            P("outer", "inner", None),
            P("outer", "inner", None),
            P("outer", "inner", None),
            P(),
        ),
        check_vma=False,
    )
```

time: 87.7 us -> 75.3 us (0.86)
  Pallas kernels: 82.4 us -> 74.5 us
  local copies, waits for them, and re-layouts: 4.36 us -> 0 us
    pallas_call x1, Pallas kernels: 82.4 us -> 72.8 us  [per_device(): pl.pallas_call(kernel, out_shape=(jax.ShapeDtypeStruct((1, TOK, ROWS), BF...]
    unnamed x7 -> x0, local copies, waits for them, and re-layouts: 3.06 us -> none
    pallas_call x0 -> x1, Pallas kernels: none -> 1.7 us  [per_device(): pl.pallas_call(deliver, out_shape=(jax.ShapeDtypeStruct((1, TOK, ROWS), B...]
    reshape x1 -> x0, local copies, waits for them, and re-layouts: 1.3 us -> none  [per_device(): return (dq, dk, dv, bias[:10].reshape(1280))]
where the time goes in v2:
time: 75.3 us; the launch traced here: 75.2 us
  Pallas kernels  74.5 us (99%)
    pallas_call x1, Pallas kernels, per_device(): pl.pallas_call(kernel, out_shape=(jax.ShapeDtypeStruct((1, TOK, ROWS), BF...  72.8 us
    pallas_call x1, Pallas kernels, per_device(): pl.pallas_call(deliver, out_shape=(jax.ShapeDtypeStruct((1, TOK, ROWS), B...  1.7 us

profile of v2, /device:TPU:1, one launch (start us, length us, event | category | flops | bytes accessed | tf_op | source)
XLA Modules:
  0.0 75.2 jit_solution(8226874881733071569)
XLA Ops:
  0.6 72.8 %shard_map.102 = (bf16[1,128,1024]{2,1,0:T(8,128)(2,1)}, bf16[1,128,128]{2,1,0:T(8,128)(2,1)}, bf16[1,128,128]{2,1,0:T(8,128)(2,1)}, f32[10,1,128]{2,1,0:T(1,128)}) custom-call(bf16[1,128,1024]{2,1,0:T(8,128)(2,1)} %q_hbm.1, bf16[1,128,128]{2,1,0:T(8,128)(2,1)} %k_hbm.1, bf16[1,128,128]{2,1,0:T(8,128)(2,1)} %v_hbm.1, bf16[1,128,1024]{2,1,0:T(8,128)(2,1)} %g_hbm.1, ...), custom_call_target="tpu_custom_call" | custom-call | tf_op jit(solution)/shard_map/pallas_call | solution.py:507
  73.5 1.7 %shard_map.103 = (bf16[1,128,1024]{2,1,0:T(8,128)(2,1)}, bf16[1,128,128]{2,1,0:T(8,128)(2,1)}, bf16[1,128,128]{2,1,0:T(8,128)(2,1)}, f32[1280]{0:T(1024)}) custom-call(bf16[1,128,1024]{2,1,0:T(8,128)(2,1)} %get-tuple-element.8.dq_in, bf16[1,128,128]{2,1,0:T(8,128)(2,1)} %get-tuple-element.9.dk_in, bf16[1,128,128]{2,1,0:T(8,128)(2,1)} %get-tuple-element.10.dv_in, ...), custom_call_target="tpu_custom_call" | custom-call | tf_op jit(solution)/shard_map/pallas_call | solution.py:522

commit v3 on v2

--- a/solution.py
+++ b/solution.py
@@ -139,33 +139,39 @@
 
     pl.semaphore_wait(barrier, 46)
 
-    def block(p, s, r, source, device):
-        return remote(
-            kv.at[source], kv.at[p, s, r], gather_send.at[p, s, r], gather_recv.at[p, s, r], device
-        )
-
-    def along_a(p, r):
-        return block(p, 0, r, (p, 0, 0), me.near(r, 0))
-
-    def along_b(p, s, r):
-        return block(p, s, r, (p, 0, r), me.near(0, s))
-
-    def across():
-        return block(1, 0, 0, (0, 0, 0), me.near(0, 0, 8))
-
-    def open_plane(p):
+    pieces = ((None,), (0, 1))
+
+    def block(p, s, r, v, source, device):
+        at = (source, (p, s, r)) if v is None else (source + (v,), (p, s, r, v))
+        sem = (p, s, r, 0 if v is None else v)
+        return remote(
+            kv.at[at[0]], kv.at[at[1]], gather_send.at[sem], gather_recv.at[sem], device
+        )
+
+    def along_a(p, r, v):
+        return block(p, 0, r, v, (p, 0, 0), me.near(r, 0))
+
+    def along_b(p, s, r, v):
+        return block(p, s, r, v, (p, 0, r), me.near(0, s))
+
+    def across(v):
+        return block(1, 0, 0, v, (0, 0, 0), me.near(0, 0, 8))
+
+    def open_plane(p, v):
         for r in (2, 1, 3):
-            along_a(p, r).start()
+            along_a(p, r, v).start()
         for s in (2, 1, 3):
-            along_b(p, s, 0).start()
+            along_b(p, s, 0, v).start()
 
     def pass_on(p, r):
-        along_a(p, r).wait_recv()
-        for s in (2, 1, 3):
-            along_b(p, s, r).start()
-
-    across().start()
-    open_plane(0)
+        for v in pieces[p]:
+            along_a(p, r, v).wait_recv()
+            for s in (2, 1, 3):
+                along_b(p, s, r, v).start()
+
+    for v in pieces[1]:
+        across(v).start()
+    open_plane(0, None)
 
     for load in loads[4:]:
         load.wait()
@@ -232,7 +238,8 @@
                 if p == 0:
                     pass_on(1, s)
                 for r in (0, 1, 3, 2):
-                    along_b(p, s, r).wait_recv()
+                    for v in pieces[p]:
+                        along_b(p, s, r, v).wait_recv()
 
             first_pass(p, s, 1 if p == 1 else jnp.minimum(t, 1))
 
@@ -240,8 +247,9 @@
 
                 @pl.when(t == 0)
                 def _():
-                    across().wait_recv()
-                    open_plane(1)
+                    for v in pieces[1]:
+                        across(v).wait_recv()
+                        open_plane(1, v)
 
             return carry
 
@@ -259,14 +267,18 @@
     d_run[...] = jnp.broadcast_to(delta, d_run.shape)
 
     def second_pass(p, s, with_v, with_k):
-        share = jnp.exp2(m_all[p, s] - m_run[...]) * l_run[...]
+        if with_v:
+            share = jnp.exp2(m_all[p, s] - m_run[...]) * l_run[...]
         for t in range(2):
             low = []
             ds = []
             for r in (2 * t, 2 * t + 1):
-                probs = e_all[p, s, r].astype(F32) * share
+                probs = e_all[p, s, r].astype(F32)
                 if with_v:
+                    probs = probs * share
                     low.append(probs.astype(BF))
+                    if not with_k:
+                        e_all[p, s, r] = low[-1]
                 if with_k:
                     ds.append((probs * (dp_all[p, s, r] - d_run[...])).astype(BF))
             if with_v:
@@ -413,13 +425,21 @@
 
     each_row(lambda j: plane_copy(j).start())
     add_b(1, 0)
-    for v in (1, 0):
-        back_b(0, 1, v).start()
-        back_b(0, 3, v).start()
+    for s in (1, 3):
+        for v in (1, 0):
+            back_b(0, s, v).start()
     fin[1] = add_a(1, 1).astype(BF)
     back_z(1).start()
     dq_copy = pltpu.make_async_copy(dq_out, dq_ref.at[0], out_sem.at[0])
     dq_copy.start()
+    for v in pieces[1]:
+        across(v).wait_send()
+    for p in range(2):
+        for r in (1, 2, 3):
+            for v in pieces[p]:
+                along_a(p, r, v).wait_send()
+                for s in range(4):
+                    along_b(p, r, s, v).wait_send()
 
     @pl.when(adds)
     def _():
@@ -433,6 +453,10 @@
     back_z(0).start()
     add_b(0, 1)
     add_b(0, 0)
+    for r in (1, 2, 3):
+        for v in range(2):
+            back_a(1, r, v).wait_send()
+            back_b(1, r, v).wait_send()
 
     @pl.when(adds)
     def _():
@@ -456,15 +480,10 @@
     dk_copy.wait()
     dv_copy.wait()
 
-    across().wait_send()
-    for p in range(2):
-        for r in (1, 2, 3):
-            along_a(p, r).wait_send()
-            for v in range(2):
-                back_a(p, r, v).wait_send()
-                back_b(p, r, v).wait_send()
-            for s in range(4):
-                along_b(p, r, s).wait_send()
+    for r in (1, 2, 3):
+        for v in range(2):
+            back_a(0, r, v).wait_send()
+            back_b(0, r, v).wait_send()
     for v in range(2):
         back_z(v).wait_send()
     each_row(lambda j: plane_copy(j).wait_send())
@@ -501,7 +520,7 @@
         low(2, 3, 2, DH, TOK), low(2, DH, TOK), low(2, DH, TOK), full(2, DH, TOK),
         low(TOK, ROWS), full(2, DH, TOK), low(2, TOK, DH),
         full(10, 1, DH), full(32, 1, DH), full(1, DH), full(16, 1, DH), full(10, 1, DH),
-        dma(7), dma(3), dma(2, 4, 4), dma(2, 4, 4), dma(2, 3, 2), dma(2, 3, 2), dma(2, 3, 2),
+        dma(7), dma(3), dma(2, 4, 4, 2), dma(2, 4, 4, 2), dma(2, 3, 2), dma(2, 3, 2), dma(2, 3, 2),
         dma(2, 3, 2), dma(2, 2), dma(10), dma(32), dma(16), dma(16), dma(32), dma(10),
     ]
     dq, dk, dv, bias = pl.pallas_call(

time: 75.3 us -> 75 us (level)
  no operation moved by 1% of the time
where the time goes in v3:
time: 75 us; the launch traced here: 74.9 us
  Pallas kernels  74.2 us (99%)
    pallas_call x1, Pallas kernels, per_device(): pl.pallas_call(kernel, out_shape=(jax.ShapeDtypeStruct((1, TOK, ROWS), BF...  72.5 us
    pallas_call x1, Pallas kernels, per_device(): pl.pallas_call(deliver, out_shape=(jax.ShapeDtypeStruct((1, TOK, ROWS), B...  1.7 us

profile of v3, /device:TPU:1, one launch (start us, length us, event | category | flops | bytes accessed | tf_op | source)
XLA Modules:
  0.0 74.9 jit_solution(10375230577172709106)
XLA Ops:
  0.6 72.5 %shard_map.102 = (bf16[1,128,1024]{2,1,0:T(8,128)(2,1)}, bf16[1,128,128]{2,1,0:T(8,128)(2,1)}, bf16[1,128,128]{2,1,0:T(8,128)(2,1)}, f32[10,1,128]{2,1,0:T(1,128)}) custom-call(bf16[1,128,1024]{2,1,0:T(8,128)(2,1)} %q_hbm.1, bf16[1,128,128]{2,1,0:T(8,128)(2,1)} %k_hbm.1, bf16[1,128,128]{2,1,0:T(8,128)(2,1)} %v_hbm.1, bf16[1,128,1024]{2,1,0:T(8,128)(2,1)} %g_hbm.1, ...), custom_call_target="tpu_custom_call" | custom-call | tf_op jit(solution)/shard_map/pallas_call | solution.py:526
  73.2 1.7 %shard_map.103 = (bf16[1,128,1024]{2,1,0:T(8,128)(2,1)}, bf16[1,128,128]{2,1,0:T(8,128)(2,1)}, bf16[1,128,128]{2,1,0:T(8,128)(2,1)}, f32[1280]{0:T(1024)}) custom-call(bf16[1,128,1024]{2,1,0:T(8,128)(2,1)} %get-tuple-element.8.dq_in, bf16[1,128,128]{2,1,0:T(8,128)(2,1)} %get-tuple-element.9.dk_in, bf16[1,128,128]{2,1,0:T(8,128)(2,1)} %get-tuple-element.10.dv_in, ...), custom_call_target="tpu_custom_call" | custom-call | tf_op jit(solution)/shard_map/pallas_call | solution.py:541
